TPU v7x, 128 devices: a whole 4x4x4 slice. The times are simulated.
128 devices in a mesh: blk: 16 (over x_lo, z, core), head: 4 (over y), dp: 2 (over x_hi).
Axes of the slice: x: 4 (x_hi: 2, x_lo: 2; x = x_hi * 2 + x_lo), y: 4, z: 4, core: 2. Of those that a mesh axis runs over, the one named last changes fastest.
Arguments:
- queries: bfloat16 [10240, 2560], P(('dp', 'blk'), 'head'), parts along dimension 0, may hold values from -6 to 6
- keys: bfloat16 [10240, 2560], P(('dp', 'blk'), 'head'), parts along dimension 0, may hold values from -6 to 6
- values: bfloat16 [10240, 2560], P(('dp', 'blk'), 'head'), parts along dimension 0, may hold values from -6 to 6
- t_queries: bfloat16 [10240, 2560], P(('dp', 'blk'), 'head'), parts along dimension 0, may hold values from -6 to 6
- t_keys: bfloat16 [10240, 2560], P(('dp', 'blk'), 'head'), parts along dimension 0, may hold values from -6 to 6
- t_values: bfloat16 [10240, 2560], P(('dp', 'blk'), 'head'), parts along dimension 0, may hold values from -6 to 6
- out_weight: bfloat16 [2560, 5120], P('head'), may hold values from -6 to 6
- stream: bfloat16 [10240, 5120], P(('dp', 'blk', 'head')), parts along dimension 0, may hold values from -6 to 6
- t_stream: bfloat16 [10240, 5120], P(('dp', 'blk', 'head')), parts along dimension 0, may hold values from -6 to 6
- gate: bfloat16 [5120], replicated, may hold values from -4 to 4
- t_gate: bfloat16 [5120], replicated, may hold values from -4 to 4
Outputs:
- result: bfloat16 [10240, 5120], P(('dp', 'blk', 'head')), parts along dimension 0
- t_result: bfloat16 [10240, 5120], P(('dp', 'blk', 'head')), parts along dimension 0
There are 2 independent parts, one for each index of `dp`. A program takes and returns all parts, laid end to end along the dimension named above; an argument that names none is the same for every part. Nothing has to cross between parts.
All inputs are finite; a program needn't handle non-finite values.
Results may differ from a plain program's by a relative error of at most 0.04.
Values may be sent and summed in bfloat16 or wider, within the bound.
No kernel may reach another device: no remote copies, remote signals or barrier semaphores. Data moves between devices by JAX's collectives and lax.ppermute only.
A program may use at most 128 MiB of HBM per device.

v0:
```python
import functools

import jax
import jax.numpy as jnp
from jax import lax
from jax.experimental import pallas as pl
from jax.experimental.pallas import tpu as pltpu
from jax.sharding import Mesh
from jax.sharding import PartitionSpec as P

HD = 128
LOG2E = 1.4426950408889634
SCALE = HD**-0.5
CHUNK = 512
SIZES = {"xl": 2, "z": 4, "core": 2, "head": 4}
WIDE = 640
VMEM = 60 * 1024 * 1024


def shift(value, axis, step):
    size = SIZES[axis]
    return lax.ppermute(value, axis, [(i, (i + step) % size) for i in range(size)])


def swap_parts(value):
    return lax.ppermute(value, ("xl", "dp"), [(1, 2), (2, 1), (3, 0), (0, 3)])


def attend_kernel(sent, *refs):
    count = len(sent)
    queries, kv = refs[:count], refs[count]
    *outs, kk, vv, scores = refs[count + 1 :]
    blocks, _, size, _ = kv.shape
    keys = blocks * size
    for i in range(blocks):
        kk[i * size : (i + 1) * size, :] = kv[i, 0, :, : 2 * HD]
        vv[i * size : (i + 1) * size, :] = kv[i, 0, :, 2 * HD :]
    across = (((1,), (1,)), ((), ()))
    size = queries[0].shape[1]
    rows = count * size
    query = jnp.concatenate([q[0, :, :HD] for q in queries], axis=0)
    mixed = jnp.concatenate([q[0, :, HD:] for q in queries], axis=0)
    mixed = jnp.concatenate([mixed, query], axis=1)
    peak = None
    for c in range(0, keys, CHUNK):
        s = lax.dot_general(
            query, kk[c : c + CHUNK, :HD], across, preferred_element_type=jnp.float32
        )
        scores[:, c : c + CHUNK] = s
        for lane in range(0, CHUNK, 128):
            part = s[:, lane : lane + 128]
            peak = part if peak is None else jnp.maximum(peak, part)
    top = jnp.max(peak, axis=1, keepdims=True) * (SCALE * LOG2E)
    den = jnp.zeros((rows, 128), jnp.float32)
    mass = jnp.zeros((rows, 128), jnp.float32)
    wide = jnp.zeros((rows, 2 * HD), jnp.float32)
    tilt = jnp.zeros((rows, HD), jnp.float32)
    for c in range(0, keys, CHUNK):
        slope = lax.dot_general(
            mixed, kk[c : c + CHUNK, :], across, preferred_element_type=jnp.float32
        )
        w = jnp.exp2(scores[:, c : c + CHUNK] * (SCALE * LOG2E) - top)
        g = w * slope
        for lane in range(0, CHUNK, 128):
            den = den + w[:, lane : lane + 128]
            mass = mass + g[:, lane : lane + 128]
        wide = wide + jnp.dot(
            w.astype(jnp.bfloat16), vv[c : c + CHUNK, :], preferred_element_type=jnp.float32
        )
        tilt = tilt + jnp.dot(
            g.astype(jnp.bfloat16), vv[c : c + CHUNK, :HD], preferred_element_type=jnp.float32
        )
    den = jnp.sum(den, axis=1, keepdims=True)
    inverse = 1.0 / den
    mean = jnp.sum(mass, axis=1, keepdims=True) * (inverse * SCALE)
    out = wide[:, :HD] * inverse
    t_out = (tilt * SCALE + wide[:, HD:]) * inverse - mean * out
    lane = lax.broadcasted_iota(jnp.int32, (rows, 128), 1)
    both = jnp.where(lane == 0, top + jnp.log2(den), mean)
    outs = list(outs)
    for i, goes in enumerate(sent):
        mine = slice(i * size, (i + 1) * size)
        ref = outs.pop(0)
        ref[0, :size, :HD] = out[mine].astype(ref.dtype)
        ref[0, :size, HD:] = t_out[mine].astype(ref.dtype)
        stats = jnp.transpose(both[mine])
        if not goes:
            outs.pop(0)[0] = stats[:8, :]
            continue
        stats = stats[:2, :]
        high = stats.astype(jnp.bfloat16).astype(jnp.float32)
        middle = (stats - high).astype(jnp.bfloat16).astype(jnp.float32)
        low = stats - high - middle
        terms = jnp.concatenate([high, middle, low, jnp.zeros_like(low)], axis=0)
        over = 2 * HD
        rest = jnp.concatenate(
            [terms[:, over:], jnp.zeros((8, 2 * over - size), jnp.float32)], axis=1
        )
        ref[0, size:, :] = jnp.concatenate([terms[:, :over], rest], axis=0).astype(jnp.bfloat16)


def attend(queries, first, kv, sent):
    rows = queries[0].shape[1]
    blocks, heads, size, _ = kv.shape
    keys = blocks * size

    def spec(r, c, at=0):
        return pl.BlockSpec((1, r, c), lambda h: (h + at, 0, 0))

    specs, shapes = [], []
    for goes in sent:
        if goes:
            specs += [spec(rows + 16, 2 * HD)]
            shapes += [jax.ShapeDtypeStruct((heads, rows + 16, 2 * HD), jnp.bfloat16)]
        else:
            specs += [spec(rows, 2 * HD), spec(8, rows)]
            shapes += [
                jax.ShapeDtypeStruct((heads, rows, 2 * HD), jnp.float32),
                jax.ShapeDtypeStruct((heads, 8, rows), jnp.float32),
            ]
    total = len(sent) * rows
    return pl.pallas_call(
        functools.partial(attend_kernel, sent),
        grid=(heads,),
        in_specs=[spec(rows, 2 * HD, first)] * len(sent)
        + [pl.BlockSpec((blocks, 1, size, 4 * HD), lambda h: (0, h, 0, 0))],
        out_specs=specs,
        out_shape=shapes,
        scratch_shapes=[
            pltpu.VMEM((keys, 2 * HD), jnp.bfloat16),
            pltpu.VMEM((keys, 2 * HD), jnp.bfloat16),
            pltpu.VMEM((total, keys), jnp.float32),
        ],
        compiler_params=pltpu.CompilerParams(vmem_limit_bytes=VMEM),
        cost_estimate=pl.CostEstimate(
            flops=heads * total * keys * HD * 12, bytes_accessed=1000, transcendentals=0
        ),
    )(*queries, kv)


def merge_kernel(me_ref, near_ref, near_stat, far_ref, *refs):
    before, (*outs, both) = refs[:-5], refs[-5:]
    heads, count, _ = near_ref.shape
    for h in range(heads):
        lse_a, mean_a = near_stat[h, 0:1, :], near_stat[h, 1:2, :]
        terms = far_ref[h, count:, :].astype(jnp.float32)
        terms = jnp.concatenate([terms[:8], terms[8:, : count - 2 * HD]], axis=1)
        lse_b = terms[0:1] + terms[2:3] + terms[4:5]
        mean_b = terms[1:2] + terms[3:4] + terms[5:6]
        top = jnp.maximum(lse_a, lse_b)
        wa = jnp.exp2(lse_a - top)
        wb = jnp.exp2(lse_b - top)
        inverse = 1.0 / (wa + wb)
        wa = wa * inverse
        wb = wb * inverse
        mean = wa * mean_a + wb * mean_b
        terms = [wa, wb, wa * (mean_a - mean), wb * (mean_b - mean)]
        terms = jnp.transpose(jnp.concatenate(terms + terms, axis=0))
        wa, wb, da, db = (terms[:, i : i + 1] for i in range(4))
        near = near_ref[h]
        far = far_ref[h, :count, :].astype(jnp.float32)
        oa, ob = near[:, :HD], far[:, :HD]
        out = wa * oa + wb * ob
        t_out = wa * near[:, HD:] + wb * far[:, HD:] + da * oa + db * ob
        both[0, :, h * HD : (h + 1) * HD] = out.astype(both.dtype)
        both[1, :, h * HD : (h + 1) * HD] = t_out.astype(both.dtype)
    rows = outs[0].shape[1]
    for step in range(4):
        at = pl.multiple_of(lax.rem(me_ref[0] + step, 4) * rows, 16)
        done = 0
        if before:
            done = before[step].shape[2]
            outs[step][:, :, :done] = before[step][...]
        outs[step][:, :, done:] = both[:, pl.ds(at, rows), :]


def merge(me, near, near_stat, far, *before):
    heads, rows, _ = near.shape
    width = heads * HD + (before[0].shape[2] if before else 0)
    whole = pl.BlockSpec(memory_space=pltpu.VMEM)
    return pl.pallas_call(
        merge_kernel,
        in_specs=[pl.BlockSpec(memory_space=pltpu.SMEM)] + [whole] * (3 + len(before)),
        out_specs=[whole] * 4,
        out_shape=[jax.ShapeDtypeStruct((2, rows // 4, width), jnp.bfloat16)] * 4,
        scratch_shapes=[pltpu.VMEM((2, rows, heads * HD), jnp.bfloat16)],
        compiler_params=pltpu.CompilerParams(vmem_limit_bytes=VMEM),
        cost_estimate=pl.CostEstimate(flops=1000, bytes_accessed=1000, transcendentals=0),
    )(me, near, near_stat, far, *before)


def pack_kernel(cut, q, t_q, k, t_k, v, t_v, first_ref, second_ref, q_ref):
    heads = q.shape[1] // HD
    for h in range(heads):
        cols = slice(h * HD, (h + 1) * HD)
        out, at = (first_ref, h) if h < cut else (second_ref, h - cut)
        for i, ref in enumerate((k, t_k, v, t_v)):
            out[at, :, i * HD : (i + 1) * HD] = ref[:, cols]
        q_ref[h, :, :HD] = q[:, cols]
        q_ref[h, :, HD:] = t_q[:, cols]


def pack(cut, *arrays):
    rows, width = arrays[0].shape
    heads = width // HD
    whole = pl.BlockSpec(memory_space=pltpu.VMEM)
    return pl.pallas_call(
        functools.partial(pack_kernel, cut),
        in_specs=[whole] * 6,
        out_specs=[whole] * 3,
        out_shape=[
            jax.ShapeDtypeStruct((cut, rows, 4 * HD), jnp.bfloat16),
            jax.ShapeDtypeStruct((heads - cut, rows, 4 * HD), jnp.bfloat16),
            jax.ShapeDtypeStruct((heads, rows, 2 * HD), jnp.bfloat16),
        ],
        compiler_params=pltpu.CompilerParams(vmem_limit_bytes=VMEM),
        cost_estimate=pl.CostEstimate(flops=1000, bytes_accessed=1000, transcendentals=0),
    )(*arrays)


def project_kernel(parts, place_ref, *refs):
    atts, refs = refs[:parts], refs[parts:]
    stream, t_stream, gate, t_gate, weight = refs[:5]
    pieces = refs[5:21]
    result, t_result, att, narrow, broad, sems = refs[21:]
    rows = stream.shape[0]
    depth = weight.shape[0]
    core = place_ref[0]
    steps = []
    for chunk, lot, count in ((1, 1, 3), (0, 0, 1)):
        for half in range(2):
            mine = pieces[8 * half : 8 * half + 8]
            far = mine[4:]
            slot = (narrow, broad)[chunk].at[half]
            sem = sems.at[2 * half + chunk]
            col = pl.multiple_of((lax.rem(core + half, 2) * 4 + lot) * WIDE, WIDE)
            sources = (weight.at[:, pl.ds(col, count * WIDE)], *mine[2 * chunk : 2 * chunk + 2])
            group = [
                pltpu.make_async_copy(source, slot.at[pl.ds(i * depth, depth), :], sem.at[i])
                for i, source in enumerate(sources)
            ]
            for move in group:
                move.start()
            for j in range(count):
                to = slot.at[pl.ds(3 * depth, depth), pl.ds(j * WIDE, WIDE)]
                for i in range(4):

                    @pl.when(place_ref[1 + i] == lot + j)
                    def _():
                        pltpu.make_async_copy(far[i], to, sem.at[3 + j]).start()

                group.append(pltpu.make_async_copy(far[0], to, sem.at[3 + j]))
            steps.append((slot, col, count * WIDE, group))
    at = 0
    for ref in atts:
        size = ref.shape[2]
        att[:rows, at : at + size] = ref[0]
        att[rows:, at : at + size] = ref[1]
        at += size
    for slot, col, width, group in steps:
        for move in group:
            move.wait()
        sums = jnp.dot(att[...], slot[...], preferred_element_type=jnp.float32)
        branch, t_branch = sums[:rows], sums[rows:]
        cols = pl.ds(col, width)
        g = gate[:, cols].astype(jnp.float32)
        tg = t_gate[:, cols].astype(jnp.float32)
        result[:, cols] = (stream[:, cols].astype(jnp.float32) + g * branch).astype(result.dtype)
        t_result[:, cols] = (
            t_stream[:, cols].astype(jnp.float32) + tg * branch + g * t_branch
        ).astype(t_result.dtype)


def project(place, atts, stream, t_stream, gate, t_gate, weight, pieces):
    rows, columns = stream.shape
    depth = weight.shape[0]
    whole = pl.BlockSpec(memory_space=pltpu.VMEM)
    away = pl.BlockSpec(memory_space=pl.ANY)
    return pl.pallas_call(
        functools.partial(project_kernel, len(atts)),
        in_specs=[pl.BlockSpec(memory_space=pltpu.SMEM)]
        + [whole] * (len(atts) + 4)
        + [away] * (1 + len(pieces)),
        out_specs=[whole] * 2,
        out_shape=[jax.ShapeDtypeStruct((rows, columns), stream.dtype)] * 2,
        scratch_shapes=[
            pltpu.VMEM((2 * rows, 4 * depth), jnp.bfloat16),
            pltpu.VMEM((2, 4 * depth, WIDE), jnp.bfloat16),
            pltpu.VMEM((2, 4 * depth, 3 * WIDE), jnp.bfloat16),
            pltpu.SemaphoreType.DMA((4, 6)),
        ],
        compiler_params=pltpu.CompilerParams(vmem_limit_bytes=VMEM),
        cost_estimate=pl.CostEstimate(flops=1000, bytes_accessed=1000, transcendentals=0),
    )(place, *atts, stream, t_stream, gate, t_gate, weight, *pieces)


def on_device(
    queries, keys, values, t_queries, t_keys, t_values, out_weight, stream, t_stream, gate, t_gate
):
    heads = queries.shape[1] // HD
    depth = out_weight.shape[0]
    half_width = out_weight.shape[1] // 2
    cut = heads - 1
    core, side, me = lax.axis_index("core"), lax.axis_index("xl"), lax.axis_index("head")
    x = 2 * lax.axis_index("dp") + side
    places = [x, x ^ 1, 3 - x, 3 - (x ^ 1)]

    def quarter(place, count=1):
        return lax.dynamic_slice(
            out_weight, (0, core * half_width + place * WIDE), (depth, count * WIDE)
        )

    def tie(value, *earlier):
        return lax.optimization_barrier((value, *earlier))[0]

    def neighbours(lot, *earlier, count=1):
        value = quarter(lot, count)
        if earlier:
            value = tie(value, *earlier)
        return shift(value, "head", 1), shift(value, "head", -1)

    def other_core(*pieces):
        return [shift(piece, "core", 1) for piece in pieces]

    lot_a, lot_b, near_q = pack(cut, queries, t_queries, keys, t_keys, values, t_values)
    kv_a = lax.all_gather(lot_a, ("z", "core"))
    kv_b = lax.all_gather(lot_b, ("z", "core"))
    far_q = shift(near_q, "xl", 1)
    gates = gate.reshape(1, -1), t_gate.reshape(1, -1)
    place = jnp.stack([core, *places]).astype(jnp.int32)
    where = me.astype(jnp.int32).reshape(1)

    far0 = tie(shift(quarter(places[0]), "head", 2), far_q)
    first = neighbours(0)
    far1, far2 = shift(far0, "xl", 1), swap_parts(far0)
    second = neighbours(1, *first, far1, far2, count=3)
    first2, fars = other_core(*first), other_core(far0)
    far3 = swap_parts(far1)

    (far_a,) = attend(
        [tie(far_q, *first2, *fars, *gates, place, where)], 0, kv_a, [True]
    )
    sent_a = shift(far_a, "xl", 1)
    near_a = attend([tie(near_q, far_a, far1, far2)], 0, kv_a, [False])
    fars += other_core(*tie((far1, far2), far_a))
    last = tie(far_q, near_a[1], far3, *fars)
    far_b, *near_b = attend([last, near_q], cut, kv_b, [True, False])
    sent_b = shift(far_b, "xl", 1)
    fars += other_core(tie(far3, far_b))
    owners_a = merge(tie(where, far_b), *near_a, sent_a)
    owners = merge(tie(where, *fars), *near_b, sent_b, *owners_a)
    second2 = other_core(*tie(second, owners_a[0], sent_b))
    moved = [owners[0]] + [shift(owners[step], "head", step) for step in (1, 2, 3)]
    atts = [moved[step] for step in (0, 1, 3, 2)]
    pieces = [*first, *second, far0, far1, far2, far3, *first2, *second2, *fars]
    return project(place, atts, stream, t_stream, *gates, out_weight, pieces)


def solution(mesh):
    fine = Mesh(
        mesh.devices.reshape(SIZES["xl"], SIZES["z"], SIZES["core"], SIZES["head"], -1),
        ("xl", "z", "core", "head", "dp"),
    )
    tokens = ("dp", "xl", "z", "core")
    spread = P(tokens, "head")
    rows = P((*tokens, "head"), None)
    return jax.shard_map(
        on_device,
        mesh=fine,
        in_specs=(spread,) * 6 + (P("head", None), rows, rows, P(), P()),
        out_specs=(rows, rows),
        check_vma=False,
    )
```

profile of v0, /device:TPU:1, one launch (start us, length us, event | category | flops | bytes accessed | tf_op | source)
XLA Modules:
  0.0 163.1 jit_solution(10296292440684589694)
XLA Ops:
  7.2 0.0 all-gather.5.cloned.1.call-start
  7.2 3.5 %shard_map.122 = (bf16[4,320,512]{2,1,0:T(8,128)(2,1)}, bf16[1,320,512]{2,1,0:T(8,128)(2,1)}, bf16[5,320,256]{2,1,0:T(8,128)(2,1)}) custom-call(bf16[320,640]{1,0:T(8,128)(2,1)} %q.1, bf16[320,640]{1,0:T(8,128)(2,1)} %t_q.1, bf16[320,640]{1,0:T(8,128)(2,1)} %k.1, bf16[320,640]{1,0:T(8,128)(2,1)} %t_k.1, bf16[320,640]{1,0:T(8,128)(2,1)} %v.1, ...), custom_call_target="tpu_custom_call" | custom-call | flops 1000 | bytes 1000 | tf_op jit(solution)/shard_map/pallas_call | solution.py:207
  10.7 0.0 all-gather.5.cloned.1.call-update
  10.7 0.0 all-gather.7.cloned.1.call-start
  10.8 0.7 all-gather.7.cloned.1.call-update
  11.5 1.6 constant_dynamic-slice_fusion.1
  13.1 3.8 %collective-permute-start = (bf16[640,640]{1,0:T(8,128)(2,1)S(1)}, bf16[640,640]{1,0:T(8,128)(2,1)S(1)}, u32[]{:S(2)}, u32[]{:S(2)}) collective-permute-start(bf16[640,640]{1,0:T(8,128)(2,1)S(1)} %get-tuple-element.59), channel_id=1, source_target_pairs={{0,4},{2,6},{4,0},{6,2},{1,5},{3,7},{5,1},{7,3},{8,12},{10,14},{12... | collective-permute-start | bytes 2457608 | tf_op jit(solution)/shard_map/ppermute | solution.py:22
  16.9 1.1 collective-permute-start.1
  18.1 0.4 collective-permute-start.5
  18.5 2.3 %collective-permute-start.7 = (bf16[640,640]{1,0:T(8,128)(2,1)S(1)}, bf16[640,640]{1,0:T(8,128)(2,1)}, u32[]{:S(2)}, u32[]{:S(2)}) collective-permute-start(bf16[640,640]{1,0:T(8,128)(2,1)S(1)} %get-tuple-element.58), channel_id=1, source_target_pairs={{0,6},{2,0},{4,2},{6,4},{1,7},{3,1},{5,3},{7,5},{8,14},{10,8},{12,... | collective-permute-start | bytes 2457608 | tf_op jit(solution)/shard_map/ppermute | solution.py:22
  20.7 13.9 %collective-permute-done.refs_13_ = bf16[640,640]{1,0:T(8,128)(2,1)S(1)} collective-permute-done((bf16[640,640]{1,0:T(8,128)(2,1)S(1)}, bf16[640,640]{1,0:T(8,128)(2,1)S(1)}, u32[]{:S(2)}, u32[]{:S(2)}) %collective-permute-start) | collective-permute-done | bytes 819232 | tf_op jit(solution)/shard_map/ppermute | solution.py:22
  34.7 1.2 collective-permute-done.1.refs_0_
  35.8 1.1 collective-permute-start.3
  37.0 1.8 %collective-permute-start.4 = (bf16[640,640]{1,0:T(8,128)(2,1)S(1)}, bf16[640,640]{1,0:T(8,128)(2,1)}, u32[]{:S(2)}, u32[]{:S(2)}) collective-permute-start(bf16[640,640]{1,0:T(8,128)(2,1)S(1)} %collective-permute-done.refs_13_), channel_id=1, source_target_pairs={{1,64},{64,1},{65,0},{0,65},{3,66},{66,3},{67,2},{2,67},{5,68},{68... | collective-permute-start | bytes 2457608 | tf_op jit(solution)/shard_map/ppermute | solution.py:26
  38.8 2.3 %collective-permute-start.2 = (bf16[640,640]{1,0:T(8,128)(2,1)S(1)}, bf16[640,640]{1,0:T(8,128)(2,1)}, u32[]{:S(2)}, u32[]{:S(2)}) collective-permute-start(bf16[640,640]{1,0:T(8,128)(2,1)S(1)} %collective-permute-done.refs_13_), channel_id=1, source_target_pairs={{0,8},{8,0},{1,9},{9,1},{2,10},{10,2},{3,11},{11,3},{4,12},{12,4},... | collective-permute-start | bytes 2457608 | tf_op jit(solution)/shard_map/ppermute | solution.py:22
  41.1 12.2 %collective-permute-done.5.refs_9_ = bf16[640,640]{1,0:T(8,128)(2,1)} collective-permute-done((bf16[640,640]{1,0:T(8,128)(2,1)S(1)}, bf16[640,640]{1,0:T(8,128)(2,1)}, u32[]{:S(2)}, u32[]{:S(2)}) %collective-permute-start.5) | collective-permute-done | bytes 819232 | tf_op jit(solution)/shard_map/ppermute | solution.py:22
  53.3 0.5 collective-permute-start.6
  53.8 0.0 collective-permute-done.7.refs_10_
  53.8 0.4 collective-permute-start.8
  54.2 1.9 %constant_dynamic-slice_fusion = bf16[640,1920]{1,0:T(8,128)(2,1)S(1)} fusion(bf16[640,5120]{1,0:T(8,128)(2,1)} %refs_8_.1, s32[]{:T(128)S(6)} %select_n.11), kind=kLoop, calls=%fused_computation | loop fusion | bytes 4915204 | tf_op jit(solution)/shard_map/dynamic_slice | solution.py:309
  56.1 0.0 collective-permute-done.3.refs_14_
  56.2 0.0 collective-permute-done.4.refs_15_
  56.2 1.2 collective-permute-start.18
  57.4 1.5 collective-permute-start.19
  58.9 0.6 reshape.14.refs_6_
  59.5 0.6 reshape.15.refs_7_
  60.1 0.7 stack.23.place_ref
  60.8 0.0 collective-permute-done.2.refs_21_
  60.8 0.0 collective-permute-done.6.refs_17_
  60.8 0.0 collective-permute-done.8.refs_18_
  60.8 2.5 %collective-permute-start.11 = (bf16[640,640]{1,0:T(8,128)(2,1)}, bf16[640,640]{1,0:T(8,128)(2,1)S(1)}, u32[]{:S(2)}, u32[]{:S(2)}) collective-permute-start(bf16[640,640]{1,0:T(8,128)(2,1)} %collective-permute-done.3.refs_14_), channel_id=1, source_target_pairs={{1,64},{64,1},{65,0},{0,65},{3,66},{66,3},{67,2},{2,67},{5,68},{68... | collective-permute-start | bytes 2457608 | tf_op jit(solution)/shard_map/ppermute | solution.py:26
  63.3 9.9 %all-gather.5.cloned.1.call-done = bf16[32,320,512]{2,1,0:T(8,128)(2,1)} async-done(((bf16[4,320,512]{2,1,0:T(8,128)(2,1)}), bf16[32,320,512]{2,1,0:T(8,128)(2,1)}) %all-gather.5.cloned.1.call-update) | async-done | bytes 10485776 | tf_op jit(solution)/shard_map/all_gather | solution.py:326
  73.3 12.3 %shard_map.123 = bf16[4,336,256]{2,1,0:T(8,128)(2,1)} custom-call(bf16[5,320,256]{2,1,0:T(8,128)(2,1)} %copy-done.11, bf16[8,4,320,512]{3,2,1,0:T(8,128)(2,1)} %bitcast.8), custom_call_target="tpu_custom_call" | custom-call | flops 5033164800 | bytes 1000 | tf_op jit(solution)/shard_map/pallas_call | solution.py:122
  85.6 0.3 collective-permute-start.9
  85.8 0.3 collective-permute-start.10
  86.1 0.0 collective-permute-done.11.refs_16_
  86.1 1.2 collective-permute-start.14
  87.3 12.4 %shard_map.124 = (f32[4,320,256]{2,1,0:T(8,128)}, f32[4,8,320]{2,1,0:T(8,128)}) custom-call(bf16[5,320,256]{2,1,0:T(8,128)(2,1)} %get-tuple-element.36.refs_0_.refs_1_, bf16[8,4,320,512]{3,2,1,0:T(8,128)(2,1)} %bitcast.9), custom_call_target="tpu_custom_call" | custom-call | flops 5033164800 | bytes 1000 | tf_op jit(solution)/shard_map/pallas_call | solution.py:122
  99.7 0.0 collective-permute-done.9.refs_22_
  99.7 0.0 collective-permute-done.10.refs_23_
  99.7 1.7 %all-gather.7.cloned.1.call-done = bf16[8,320,512]{2,1,0:T(8,128)(2,1)} async-done(((bf16[1,320,512]{2,1,0:T(8,128)(2,1)}), bf16[8,320,512]{2,1,0:T(8,128)(2,1)}) %all-gather.7.cloned.1.call-update) | async-done | bytes 2621456 | tf_op jit(solution)/shard_map/all_gather | solution.py:327
  101.4 7.3 %shard_map.125 = (bf16[1,336,256]{2,1,0:T(8,128)(2,1)}, f32[1,320,256]{2,1,0:T(8,128)}, f32[1,8,320]{2,1,0:T(8,128)}) custom-call(bf16[5,320,256]{2,1,0:T(8,128)(2,1)} %copy-done.11, bf16[5,320,256]{2,1,0:T(8,128)(2,1)} %get-tuple-element.36.refs_0_.refs_1_, bf16[8,1,320,512]{3,2,1,0:T(8,128)(2,1)} %bitcast.10), custom_call_target="tpu_custom_call" | custom-call | flops 2516582400 | bytes 1000 | tf_op jit(solution)/shard_map/pallas_call | solution.py:122
  108.8 1.2 collective-permute-start.13
  110.0 0.0 collective-permute-done.14.far_ref
  110.0 3.6 %shard_map.126 = (bf16[2,80,512]{2,1,0:T(8,128)(2,1)}, bf16[2,80,512]{2,1,0:T(8,128)(2,1)}, bf16[2,80,512]{2,1,0:T(8,128)(2,1)}, bf16[2,80,512]{2,1,0:T(8,128)(2,1)}) custom-call(s32[1]{0:T(128)} %bitcast.5.me_ref, f32[4,320,256]{2,1,0:T(8,128)} %get-tuple-element.46.near_ref, f32[4,8,320]{2,1,0:T(8,128)} %get-tuple-element.37.near_stat, ...), custom_call_target="tpu_custom_call" | custom-call | flops 1000 | bytes 1000 | tf_op jit(solution)/shard_map/pallas_call | solution.py:181
  113.5 0.0 collective-permute-done.18.refs_11_
  113.5 0.0 collective-permute-done.19.refs_12_
  113.5 1.1 collective-permute-done.13.far_ref
  114.7 1.1 collective-permute-start.20
  115.8 0.0 collective-permute-start.21
  115.8 0.5 collective-permute-start.12
  116.3 8.5 %collective-permute-done.12.refs_24_ = bf16[640,640]{1,0:T(8,128)(2,1)S(1)} collective-permute-done((bf16[640,640]{1,0:T(8,128)(2,1)S(1)}, bf16[640,640]{1,0:T(8,128)(2,1)S(1)}, u32[]{:S(2)}, u32[]{:S(2)}) %collective-permute-start.12) | collective-permute-done | bytes 819232 | tf_op jit(solution)/shard_map/ppermute | solution.py:22
  124.7 0.9 copy-done.3
  125.7 2.6 %shard_map.127 = (bf16[2,80,640]{2,1,0:T(8,128)(2,1)}, bf16[2,80,640]{2,1,0:T(8,128)(2,1)}, bf16[2,80,640]{2,1,0:T(8,128)(2,1)}, bf16[2,80,640]{2,1,0:T(8,128)(2,1)}) custom-call(s32[1]{0:T(128)} %bitcast.5.me_ref, f32[1,320,256]{2,1,0:T(8,128)} %get-tuple-element.43.near_ref, f32[1,8,320]{2,1,0:T(8,128)} %get-tuple-element.44.near_stat, ...), custom_call_target="tpu_custom_call" | custom-call | flops 1000 | bytes 1000 | tf_op jit(solution)/shard_map/pallas_call | solution.py:181
  128.3 1.2 collective-permute-start.15
  129.5 1.5 collective-permute-start.16
  131.0 1.5 collective-permute-start.17
  132.5 3.5 %collective-permute-done.15.refs_1_ = bf16[2,80,640]{2,1,0:T(8,128)(2,1)S(1)} collective-permute-done((bf16[2,80,640]{2,1,0:T(8,128)(2,1)}, bf16[2,80,640]{2,1,0:T(8,128)(2,1)S(1)}, u32[]{:S(2)}, u32[]{:S(2)}) %collective-permute-start.15) | collective-permute-done | bytes 204832 | tf_op jit(solution)/shard_map/ppermute | solution.py:22
  136.0 5.4 %collective-permute-done.17.refs_3_ = bf16[2,80,640]{2,1,0:T(8,128)(2,1)S(1)} collective-permute-done((bf16[2,80,640]{2,1,0:T(8,128)(2,1)}, bf16[2,80,640]{2,1,0:T(8,128)(2,1)S(1)}, u32[]{:S(2)}, u32[]{:S(2)}) %collective-permute-start.17) | collective-permute-done | bytes 204832 | tf_op jit(solution)/shard_map/ppermute | solution.py:22
  141.4 0.0 collective-permute-done.20.refs_19_
  141.4 0.0 collective-permute-done.21.refs_20_
  141.4 0.7 copy-done.6
  142.1 0.9 copy-done
  143.0 13.3 %shard_map.128 = (bf16[80,5120]{1,0:T(8,128)(2,1)}, bf16[80,5120]{1,0:T(8,128)(2,1)}) custom-call(s32[5]{0:T(128)} %stack.23.place_ref, bf16[2,80,640]{2,1,0:T(8,128)(2,1)} %get-tuple-element.51.refs_0_, bf16[2,80,640]{2,1,0:T(8,128)(2,1)} %copy-done.4, bf16[2,80,640]{2,1,0:T(8,128)(2,1)} %copy-done.5, bf16[2,80,640]{2,1,0:T(8,128)(2,1)} %copy-done.6, ...), custom_call_target="tpu_custom_call" | custom-call | flops 1000 | bytes 1000 | tf_op jit(solution)/shard_map/pallas_call | solution.py:279
  (22 shorter events, 0.0 us)
Async XLA Ops:
  7.2 66.1 %all-gather.5.cloned.1.call-start = ((), (), s32[]{:S(2)}) async-start(), calls=%async_computation | async-start | bytes 11796480 | tf_op jit(solution)/shard_map/all_gather | solution.py:326
  10.7 6.2 %copy-start.10 = (bf16[5,320,256]{2,1,0:T(8,128)(2,1)S(1)}, bf16[5,320,256]{2,1,0:T(8,128)(2,1)}, u32[]{:S(2)}) copy-start(bf16[5,320,256]{2,1,0:T(8,128)(2,1)} %get-tuple-element.36.refs_0_.refs_1_) | copy-start | bytes 2457604
  10.7 90.7 %all-gather.7.cloned.1.call-start = ((), (), s32[]{:S(2)}) async-start(), calls=%async_computation.1 | async-start | bytes 2949120 | tf_op jit(solution)/shard_map/all_gather | solution.py:327
  13.1 21.6 %collective-permute-start = (bf16[640,640]{1,0:T(8,128)(2,1)S(1)}, bf16[640,640]{1,0:T(8,128)(2,1)S(1)}, u32[]{:S(2)}, u32[]{:S(2)}) collective-permute-start(bf16[640,640]{1,0:T(8,128)(2,1)S(1)} %get-tuple-element.59), channel_id=1, source_target_pairs={{0,4},{2,6},{4,0},{6,2},{1,5},{3,7},{5,1},{7,3},{8,12},{10,14},{12... | collective-permute-start | bytes 2457608 | tf_op jit(solution)/shard_map/ppermute | solution.py:22
  16.9 18.9 %collective-permute-start.1 = (bf16[5,320,256]{2,1,0:T(8,128)(2,1)S(1)}, bf16[5,320,256]{2,1,0:T(8,128)(2,1)S(1)}, u32[]{:S(2)}, u32[]{:S(2)}) collective-permute-start(bf16[5,320,256]{2,1,0:T(8,128)(2,1)S(1)} %copy-done.10), channel_id=1, source_target_pairs={{0,64},{64,0},{1,65},{65,1},{2,66},{66,2},{3,67},{67,3},{4,68},{68... | collective-permute-start | bytes 2457608 | tf_op jit(solution)/shard_map/ppermute | solution.py:22
  18.1 35.2 %collective-permute-start.5 = (bf16[640,640]{1,0:T(8,128)(2,1)S(1)}, bf16[640,640]{1,0:T(8,128)(2,1)}, u32[]{:S(2)}, u32[]{:S(2)}) collective-permute-start(bf16[640,640]{1,0:T(8,128)(2,1)S(1)} %get-tuple-element.58), channel_id=1, source_target_pairs={{0,2},{2,4},{4,6},{6,0},{1,3},{3,5},{5,7},{7,1},{8,10},{10,12},{12... | collective-permute-start | bytes 2457608 | tf_op jit(solution)/shard_map/ppermute | solution.py:22
  18.5 35.3 %collective-permute-start.7 = (bf16[640,640]{1,0:T(8,128)(2,1)S(1)}, bf16[640,640]{1,0:T(8,128)(2,1)}, u32[]{:S(2)}, u32[]{:S(2)}) collective-permute-start(bf16[640,640]{1,0:T(8,128)(2,1)S(1)} %get-tuple-element.58), channel_id=1, source_target_pairs={{0,6},{2,0},{4,2},{6,4},{1,7},{3,1},{5,3},{7,5},{8,14},{10,8},{12,... | collective-permute-start | bytes 2457608 | tf_op jit(solution)/shard_map/ppermute | solution.py:22
  34.7 21.5 %copy-start.1 = (bf16[640,640]{1,0:T(8,128)(2,1)}, bf16[640,640]{1,0:T(8,128)(2,1)S(1)}, u32[]{:S(2)}) copy-start(bf16[640,640]{1,0:T(8,128)(2,1)S(1)} %collective-permute-done.refs_13_) | copy-start | bytes 2457604
  35.8 17.9 %copy-start.11 = (bf16[5,320,256]{2,1,0:T(8,128)(2,1)}, bf16[5,320,256]{2,1,0:T(8,128)(2,1)S(1)}, u32[]{:S(2)}) copy-start(bf16[5,320,256]{2,1,0:T(8,128)(2,1)S(1)} %collective-permute-done.1.refs_0_) | copy-start | bytes 2457604
  35.8 20.3 %collective-permute-start.3 = (bf16[640,640]{1,0:T(8,128)(2,1)S(1)}, bf16[640,640]{1,0:T(8,128)(2,1)}, u32[]{:S(2)}, u32[]{:S(2)}) collective-permute-start(bf16[640,640]{1,0:T(8,128)(2,1)S(1)} %collective-permute-done.refs_13_), channel_id=1, source_target_pairs={{0,64},{64,0},{1,65},{65,1},{2,66},{66,2},{3,67},{67,3},{4,68},{68... | collective-permute-start | bytes 2457608 | tf_op jit(solution)/shard_map/ppermute | solution.py:22
  37.0 19.2 %collective-permute-start.4 = (bf16[640,640]{1,0:T(8,128)(2,1)S(1)}, bf16[640,640]{1,0:T(8,128)(2,1)}, u32[]{:S(2)}, u32[]{:S(2)}) collective-permute-start(bf16[640,640]{1,0:T(8,128)(2,1)S(1)} %collective-permute-done.refs_13_), channel_id=1, source_target_pairs={{1,64},{64,1},{65,0},{0,65},{3,66},{66,3},{67,2},{2,67},{5,68},{68... | collective-permute-start | bytes 2457608 | tf_op jit(solution)/shard_map/ppermute | solution.py:26
  38.8 20.1 %copy-start.8 = (bf16[5120]{0:T(1024)(128)(2,1)S(1)}, bf16[5120]{0:T(1024)(128)(2,1)}, u32[]{:S(2)}) copy-start(bf16[5120]{0:T(1024)(128)(2,1)} %param.20) | copy-start | bytes 30724
  38.8 20.7 %copy-start.9 = (bf16[5120]{0:T(1024)(128)(2,1)S(1)}, bf16[5120]{0:T(1024)(128)(2,1)}, u32[]{:S(2)}) copy-start(bf16[5120]{0:T(1024)(128)(2,1)} %param.21) | copy-start | bytes 30724
  38.8 22.0 %collective-permute-start.2 = (bf16[640,640]{1,0:T(8,128)(2,1)S(1)}, bf16[640,640]{1,0:T(8,128)(2,1)}, u32[]{:S(2)}, u32[]{:S(2)}) collective-permute-start(bf16[640,640]{1,0:T(8,128)(2,1)S(1)} %collective-permute-done.refs_13_), channel_id=1, source_target_pairs={{0,8},{8,0},{1,9},{9,1},{2,10},{10,2},{3,11},{11,3},{4,12},{12,4},... | collective-permute-start | bytes 2457608 | tf_op jit(solution)/shard_map/ppermute | solution.py:22
  53.3 7.5 %collective-permute-start.6 = (bf16[640,640]{1,0:T(8,128)(2,1)}, bf16[640,640]{1,0:T(8,128)(2,1)}, u32[]{:S(2)}, u32[]{:S(2)}) collective-permute-start(bf16[640,640]{1,0:T(8,128)(2,1)} %collective-permute-done.5.refs_9_), channel_id=1, source_target_pairs={{0,8},{8,0},{1,9},{9,1},{2,10},{10,2},{3,11},{11,3},{4,12},{12,4},... | collective-permute-start | bytes 2457608 | tf_op jit(solution)/shard_map/ppermute | solution.py:22
  53.8 7.0 %collective-permute-start.8 = (bf16[640,640]{1,0:T(8,128)(2,1)}, bf16[640,640]{1,0:T(8,128)(2,1)}, u32[]{:S(2)}, u32[]{:S(2)}) collective-permute-start(bf16[640,640]{1,0:T(8,128)(2,1)} %collective-permute-done.7.refs_10_), channel_id=1, source_target_pairs={{0,8},{8,0},{1,9},{9,1},{2,10},{10,2},{3,11},{11,3},{4,12},{12,4},... | collective-permute-start | bytes 2457608 | tf_op jit(solution)/shard_map/ppermute | solution.py:22
  56.2 57.4 %collective-permute-start.18 = (bf16[640,1920]{1,0:T(8,128)(2,1)S(1)}, bf16[640,1920]{1,0:T(8,128)(2,1)}, u32[]{:S(2)}, u32[]{:S(2)}) collective-permute-start(bf16[640,1920]{1,0:T(8,128)(2,1)S(1)} %constant_dynamic-slice_fusion), channel_id=1, source_target_pairs={{0,2},{2,4},{4,6},{6,0},{1,3},{3,5},{5,7},{7,1},{8,10},{10,12},{12... | collective-permute-start | bytes 7372808 | tf_op jit(solution)/shard_map/ppermute | solution.py:22
  57.4 56.1 %collective-permute-start.19 = (bf16[640,1920]{1,0:T(8,128)(2,1)S(1)}, bf16[640,1920]{1,0:T(8,128)(2,1)}, u32[]{:S(2)}, u32[]{:S(2)}) collective-permute-start(bf16[640,1920]{1,0:T(8,128)(2,1)S(1)} %constant_dynamic-slice_fusion), channel_id=1, source_target_pairs={{0,6},{2,0},{4,2},{6,4},{1,7},{3,1},{5,3},{7,5},{8,14},{10,8},{12,... | collective-permute-start | bytes 7372808 | tf_op jit(solution)/shard_map/ppermute | solution.py:22
  60.8 25.3 %collective-permute-start.11 = (bf16[640,640]{1,0:T(8,128)(2,1)}, bf16[640,640]{1,0:T(8,128)(2,1)S(1)}, u32[]{:S(2)}, u32[]{:S(2)}) collective-permute-start(bf16[640,640]{1,0:T(8,128)(2,1)} %collective-permute-done.3.refs_14_), channel_id=1, source_target_pairs={{1,64},{64,1},{65,0},{0,65},{3,66},{66,3},{67,2},{2,67},{5,68},{68... | collective-permute-start | bytes 2457608 | tf_op jit(solution)/shard_map/ppermute | solution.py:26
  85.6 14.1 %collective-permute-start.9 = (bf16[640,640]{1,0:T(8,128)(2,1)}, bf16[640,640]{1,0:T(8,128)(2,1)}, u32[]{:S(2)}, u32[]{:S(2)}) collective-permute-start(bf16[640,640]{1,0:T(8,128)(2,1)} %collective-permute-done.3.refs_14_), channel_id=1, source_target_pairs={{0,8},{8,0},{1,9},{9,1},{2,10},{10,2},{3,11},{11,3},{4,12},{12,4},... | collective-permute-start | bytes 2457608 | tf_op jit(solution)/shard_map/ppermute | solution.py:22
  85.8 13.9 %collective-permute-start.10 = (bf16[640,640]{1,0:T(8,128)(2,1)}, bf16[640,640]{1,0:T(8,128)(2,1)}, u32[]{:S(2)}, u32[]{:S(2)}) collective-permute-start(bf16[640,640]{1,0:T(8,128)(2,1)} %collective-permute-done.4.refs_15_), channel_id=1, source_target_pairs={{0,8},{8,0},{1,9},{9,1},{2,10},{10,2},{3,11},{11,3},{4,12},{12,4},... | collective-permute-start | bytes 2457608 | tf_op jit(solution)/shard_map/ppermute | solution.py:22
  86.1 29.7 %copy-start.2 = (bf16[640,640]{1,0:T(8,128)(2,1)}, bf16[640,640]{1,0:T(8,128)(2,1)S(1)}, u32[]{:S(2)}) copy-start(bf16[640,640]{1,0:T(8,128)(2,1)S(1)} %collective-permute-done.11.refs_16_) | copy-start | bytes 2457604
  86.1 23.8 %collective-permute-start.14 = (bf16[4,336,256]{2,1,0:T(8,128)(2,1)}, bf16[4,336,256]{2,1,0:T(8,128)(2,1)}, u32[]{:S(2)}, u32[]{:S(2)}) collective-permute-start(bf16[4,336,256]{2,1,0:T(8,128)(2,1)} %shard_map.123), channel_id=1, source_target_pairs={{0,64},{64,0},{1,65},{65,1},{2,66},{66,2},{3,67},{67,3},{4,68},{68... | collective-permute-start | bytes 2064392 | tf_op jit(solution)/shard_map/ppermute | solution.py:22
  108.8 5.9 %collective-permute-start.13 = (bf16[1,336,256]{2,1,0:T(8,128)(2,1)}, bf16[1,336,256]{2,1,0:T(8,128)(2,1)S(1)}, u32[]{:S(2)}, u32[]{:S(2)}) collective-permute-start(bf16[1,336,256]{2,1,0:T(8,128)(2,1)} %get-tuple-element.40), channel_id=1, source_target_pairs={{0,64},{64,0},{1,65},{65,1},{2,66},{66,2},{3,67},{67,3},{4,68},{68... | collective-permute-start | bytes 516104 | tf_op jit(solution)/shard_map/ppermute | solution.py:22
  114.7 11.0 %copy-start.7 = (bf16[1,336,256]{2,1,0:T(8,128)(2,1)}, bf16[1,336,256]{2,1,0:T(8,128)(2,1)S(1)}, u32[]{:S(2)}) copy-start(bf16[1,336,256]{2,1,0:T(8,128)(2,1)S(1)} %collective-permute-done.13.far_ref) | copy-start | bytes 516100
  114.7 26.7 %collective-permute-start.20 = (bf16[640,1920]{1,0:T(8,128)(2,1)}, bf16[640,1920]{1,0:T(8,128)(2,1)S(1)}, u32[]{:S(2)}, u32[]{:S(2)}) collective-permute-start(bf16[640,1920]{1,0:T(8,128)(2,1)} %collective-permute-done.18.refs_11_), channel_id=1, source_target_pairs={{0,8},{8,0},{1,9},{9,1},{2,10},{10,2},{3,11},{11,3},{4,12},{12,4},... | collective-permute-start | bytes 7372808 | tf_op jit(solution)/shard_map/ppermute | solution.py:22
  115.8 25.6 %collective-permute-start.21 = (bf16[640,1920]{1,0:T(8,128)(2,1)}, bf16[640,1920]{1,0:T(8,128)(2,1)}, u32[]{:S(2)}, u32[]{:S(2)}) collective-permute-start(bf16[640,1920]{1,0:T(8,128)(2,1)} %collective-permute-done.19.refs_12_), channel_id=1, source_target_pairs={{0,8},{8,0},{1,9},{9,1},{2,10},{10,2},{3,11},{11,3},{4,12},{12,4},... | collective-permute-start | bytes 7372808 | tf_op jit(solution)/shard_map/ppermute | solution.py:22
  115.8 9.0 %collective-permute-start.12 = (bf16[640,640]{1,0:T(8,128)(2,1)S(1)}, bf16[640,640]{1,0:T(8,128)(2,1)S(1)}, u32[]{:S(2)}, u32[]{:S(2)}) collective-permute-start(bf16[640,640]{1,0:T(8,128)(2,1)S(1)} %collective-permute-done.11.refs_16_), channel_id=1, source_target_pairs={{0,8},{8,0},{1,9},{9,1},{2,10},{10,2},{3,11},{11,3},{4,12},{12,4},... | collective-permute-start | bytes 2457608 | tf_op jit(solution)/shard_map/ppermute | solution.py:22
  124.7 0.9 copy-start.3
  128.3 7.7 %collective-permute-start.15 = (bf16[2,80,640]{2,1,0:T(8,128)(2,1)}, bf16[2,80,640]{2,1,0:T(8,128)(2,1)S(1)}, u32[]{:S(2)}, u32[]{:S(2)}) collective-permute-start(bf16[2,80,640]{2,1,0:T(8,128)(2,1)} %get-tuple-element.52), channel_id=1, source_target_pairs={{0,2},{2,4},{4,6},{6,0},{1,3},{3,5},{5,7},{7,1},{8,10},{10,12},{12... | collective-permute-start | bytes 614408 | tf_op jit(solution)/shard_map/ppermute | solution.py:22
  129.5 6.5 %collective-permute-start.16 = (bf16[2,80,640]{2,1,0:T(8,128)(2,1)}, bf16[2,80,640]{2,1,0:T(8,128)(2,1)S(1)}, u32[]{:S(2)}, u32[]{:S(2)}) collective-permute-start(bf16[2,80,640]{2,1,0:T(8,128)(2,1)} %get-tuple-element.53), channel_id=1, source_target_pairs={{0,6},{2,0},{4,2},{6,4},{1,7},{3,1},{5,3},{7,5},{8,14},{10,8},{12,... | collective-permute-start | bytes 614408 | tf_op jit(solution)/shard_map/ppermute | solution.py:22
  131.0 10.4 %collective-permute-start.17 = (bf16[2,80,640]{2,1,0:T(8,128)(2,1)}, bf16[2,80,640]{2,1,0:T(8,128)(2,1)S(1)}, u32[]{:S(2)}, u32[]{:S(2)}) collective-permute-start(bf16[2,80,640]{2,1,0:T(8,128)(2,1)} %get-tuple-element.54), channel_id=1, source_target_pairs={{0,4},{2,6},{4,0},{6,2},{1,5},{3,7},{5,1},{7,3},{8,12},{10,14},{12... | collective-permute-start | bytes 614408 | tf_op jit(solution)/shard_map/ppermute | solution.py:22
  136.0 5.4 %copy-start.4 = (bf16[2,80,640]{2,1,0:T(8,128)(2,1)}, bf16[2,80,640]{2,1,0:T(8,128)(2,1)S(1)}, u32[]{:S(2)}) copy-start(bf16[2,80,640]{2,1,0:T(8,128)(2,1)S(1)} %collective-permute-done.15.refs_1_) | copy-start | bytes 614404
  136.0 5.4 %copy-start.5 = (bf16[2,80,640]{2,1,0:T(8,128)(2,1)}, bf16[2,80,640]{2,1,0:T(8,128)(2,1)S(1)}, u32[]{:S(2)}) copy-start(bf16[2,80,640]{2,1,0:T(8,128)(2,1)S(1)} %collective-permute-done.16.refs_2_) | copy-start | bytes 614404
  141.4 0.7 copy-start.6
  141.4 1.6 copy-start
Sparse Core Ops, SparseCore 0:
  10.8 62.3 all-gather.4
  74.9 26.4 all-gather.6
where the time goes:
time: 163 us
  waiting for transfers between devices  58.1 us (36%)
  Pallas kernels  55.1 us (34%)
  starting transfers between devices  27.9 us (17%)
  between operations  14.2 us (9%)
  local copies, waits for them, and re-layouts  7.9 us (5%)
    ppermute x20, waiting for transfers between devices, shift(): lax.ppermute(value, axis, [(i, (i + step) % size) for i in range(size)])  45.8 us
    pallas_call x3, Pallas kernels, attend(): pl.pallas_call(functools.partial(attend_kernel, sent), grid=(heads,), in_...  32.1 us
    ppermute x20, starting transfers between devices, shift(): lax.ppermute(value, axis, [(i, (i + step) % size) for i in range(size)])  23.5 us
    pallas_call x1, Pallas kernels, project(): pl.pallas_call(functools.partial(project_kernel, len(atts)), in_specs=[pl...  13.3 us
    all_gather x1, waiting for transfers between devices, on_device(): kv_a = lax.all_gather(lot_a, ('z', 'core'))  9.94 us
    pallas_call x2, Pallas kernels, merge(): pl.pallas_call(merge_kernel, in_specs=[pl.BlockSpec(memory_space=pltpu.SM...  6.22 us
    ppermute x2, starting transfers between devices, swap_parts(): return lax.ppermute(value, ('xl', 'dp'), [(1, 2), (2, 1), (3, 0), (0, 3)])  4.31 us
    dynamic_slice x2, local copies, waits for them, and re-layouts, quarter(): lax.dynamic_slice(out_weight, (0, core * half_width + place * WIDE), (dep...  3.53 us
  transfers between devices with their start and end apart: 24, of which 9 were waited for; matrix products, arithmetic and copies ran while one was open for 3% of the time, Pallas kernels for 23%

commit v1 on v0

--- a/solution.py
+++ b/solution.py
@@ -342,13 +342,12 @@
     )
     sent_a = shift(far_a, "xl", 1)
     near_a = attend([tie(near_q, far_a, far1, far2)], 0, kv_a, [False])
-    fars += other_core(*tie((far1, far2), far_a))
-    last = tie(far_q, near_a[1], far3, *fars)
+    fars += other_core(*tie((far1, far2, far3), far_a))
+    last = tie(far_q, near_a[1], *fars)
     far_b, *near_b = attend([last, near_q], cut, kv_b, [True, False])
     sent_b = shift(far_b, "xl", 1)
-    fars += other_core(tie(far3, far_b))
     owners_a = merge(tie(where, far_b), *near_a, sent_a)
-    owners = merge(tie(where, *fars), *near_b, sent_b, *owners_a)
+    owners = merge(where, *near_b, sent_b, *owners_a)
     second2 = other_core(*tie(second, owners_a[0], sent_b))
     moved = [owners[0]] + [shift(owners[step], "head", step) for step in (1, 2, 3)]
     atts = [moved[step] for step in (0, 1, 3, 2)]

time: 163 us -> 154 us (0.945)
  waiting for transfers between devices: 58.1 us -> 53.4 us
  starting transfers between devices: 27.9 us -> 24.4 us
    ppermute x20, starting transfers between devices: 23.5 us -> 20 us  [shift(): lax.ppermute(value, axis, [(i, (i + step) % size) for i in range(size)])]
    ppermute x20, waiting for transfers between devices: 45.8 us -> 43.5 us  [shift(): lax.ppermute(value, axis, [(i, (i + step) % size) for i in range(size)])]
    all_gather x1, waiting for transfers between devices: 1.68 us -> 0.02 us  [on_device(): kv_b = lax.all_gather(lot_b, ('z', 'core'))]
  transfers between devices with their start and end apart: 24 -> 24, of which waited for: 9 -> 9; matrix products, arithmetic and copies ran while one was open for 3% -> 4% of each run, Pallas kernels for 23% -> 25%
where the time goes in v1:
time: 154 us
  Pallas kernels  55.2 us (36%)
  waiting for transfers between devices  53.4 us (35%)
  starting transfers between devices  24.4 us (16%)
  between operations  14.2 us (9%)
  local copies, waits for them, and re-layouts  6.98 us (5%)
    ppermute x20, waiting for transfers between devices, shift(): lax.ppermute(value, axis, [(i, (i + step) % size) for i in range(size)])  43.5 us
    pallas_call x3, Pallas kernels, attend(): pl.pallas_call(functools.partial(attend_kernel, sent), grid=(heads,), in_...  32.2 us
    ppermute x20, starting transfers between devices, shift(): lax.ppermute(value, axis, [(i, (i + step) % size) for i in range(size)])  20 us
    pallas_call x1, Pallas kernels, project(): pl.pallas_call(functools.partial(project_kernel, len(atts)), in_specs=[pl...  13.3 us
    all_gather x1, waiting for transfers between devices, on_device(): kv_a = lax.all_gather(lot_a, ('z', 'core'))  9.19 us
    pallas_call x2, Pallas kernels, merge(): pl.pallas_call(merge_kernel, in_specs=[pl.BlockSpec(memory_space=pltpu.SM...  6.22 us
    ppermute x2, starting transfers between devices, swap_parts(): return lax.ppermute(value, ('xl', 'dp'), [(1, 2), (2, 1), (3, 0), (0, 3)])  4.32 us
    dynamic_slice x2, local copies, waits for them, and re-layouts, quarter(): lax.dynamic_slice(out_weight, (0, core * half_width + place * WIDE), (dep...  3.54 us
  transfers between devices with their start and end apart: 24, of which 9 were waited for; matrix products, arithmetic and copies ran while one was open for 4% of the time, Pallas kernels for 25%

profile of v1, /device:TPU:1, one launch (start us, length us, event | category | flops | bytes accessed | tf_op | source)
XLA Modules:
  0.0 154.1 jit_solution(17813323544785390594)
XLA Ops:
  7.2 0.0 all-gather.5.cloned.1.call-start
  7.2 3.5 %shard_map.122 = (bf16[4,320,512]{2,1,0:T(8,128)(2,1)}, bf16[1,320,512]{2,1,0:T(8,128)(2,1)}, bf16[5,320,256]{2,1,0:T(8,128)(2,1)}) custom-call(bf16[320,640]{1,0:T(8,128)(2,1)} %q.1, bf16[320,640]{1,0:T(8,128)(2,1)} %t_q.1, bf16[320,640]{1,0:T(8,128)(2,1)} %k.1, bf16[320,640]{1,0:T(8,128)(2,1)} %t_k.1, bf16[320,640]{1,0:T(8,128)(2,1)} %v.1, ...), custom_call_target="tpu_custom_call" | custom-call | flops 1000 | bytes 1000 | tf_op jit(solution)/shard_map/pallas_call | solution.py:207
  10.7 0.0 all-gather.5.cloned.1.call-update
  10.7 0.0 all-gather.7.cloned.1.call-start
  10.8 0.7 all-gather.7.cloned.1.call-update
  11.5 2.1 %collective-permute-start = (bf16[5,320,256]{2,1,0:T(8,128)(2,1)}, bf16[5,320,256]{2,1,0:T(8,128)(2,1)S(1)}, u32[]{:S(2)}, u32[]{:S(2)}) collective-permute-start(bf16[5,320,256]{2,1,0:T(8,128)(2,1)} %get-tuple-element.33.refs_0_.refs_1_), channel_id=1, source_target_pairs={{0,64},{64,0},{1,65},{65,1},{2,66},{66,2},{3,67},{67,3},{4,68},{68... | collective-permute-start | bytes 2457608 | tf_op jit(solution)/shard_map/ppermute | solution.py:22
  13.6 1.6 %constant_dynamic-slice_fusion.1 = (bf16[640,640]{1,0:T(8,128)(2,1)S(1)}, bf16[640,640]{1,0:T(8,128)(2,1)S(1)}) fusion(bf16[640,5120]{1,0:T(8,128)(2,1)} %refs_8_.1, s32[]{:T(128)S(6)} %select_n.10, s32[]{:T(128)S(6)} %select_n.9), kind=kLoop, calls=%fused_computation.1 | loop fusion | bytes 3276808 | tf_op jit(solution)/shard_map/dynamic_slice | solution.py:309
  15.2 3.0 %collective-permute-start.5 = (bf16[640,640]{1,0:T(8,128)(2,1)S(1)}, bf16[640,640]{1,0:T(8,128)(2,1)S(1)}, u32[]{:S(2)}, u32[]{:S(2)}) collective-permute-start(bf16[640,640]{1,0:T(8,128)(2,1)S(1)} %get-tuple-element.56), channel_id=1, source_target_pairs={{0,4},{2,6},{4,0},{6,2},{1,5},{3,7},{5,1},{7,3},{8,12},{10,14},{12... | collective-permute-start | bytes 2457608 | tf_op jit(solution)/shard_map/ppermute | solution.py:22
  18.2 0.4 collective-permute-start.1
  18.6 2.3 %collective-permute-start.3 = (bf16[640,640]{1,0:T(8,128)(2,1)S(1)}, bf16[640,640]{1,0:T(8,128)(2,1)}, u32[]{:S(2)}, u32[]{:S(2)}) collective-permute-start(bf16[640,640]{1,0:T(8,128)(2,1)S(1)} %get-tuple-element.57), channel_id=1, source_target_pairs={{0,6},{2,0},{4,2},{6,4},{1,7},{3,1},{5,3},{7,5},{8,14},{10,8},{12,... | collective-permute-start | bytes 2457608 | tf_op jit(solution)/shard_map/ppermute | solution.py:22
  20.9 10.5 %collective-permute-done.refs_0_ = bf16[5,320,256]{2,1,0:T(8,128)(2,1)S(1)} collective-permute-done((bf16[5,320,256]{2,1,0:T(8,128)(2,1)}, bf16[5,320,256]{2,1,0:T(8,128)(2,1)S(1)}, u32[]{:S(2)}, u32[]{:S(2)}) %collective-permute-start) | collective-permute-done | bytes 819232 | tf_op jit(solution)/shard_map/ppermute | solution.py:22
  31.4 4.3 %collective-permute-done.5.refs_13_ = bf16[640,640]{1,0:T(8,128)(2,1)S(1)} collective-permute-done((bf16[640,640]{1,0:T(8,128)(2,1)S(1)}, bf16[640,640]{1,0:T(8,128)(2,1)S(1)}, u32[]{:S(2)}, u32[]{:S(2)}) %collective-permute-start.5) | collective-permute-done | bytes 819232 | tf_op jit(solution)/shard_map/ppermute | solution.py:22
  35.6 0.2 collective-permute-start.7
  35.8 2.5 %collective-permute-start.8 = (bf16[640,640]{1,0:T(8,128)(2,1)S(1)}, bf16[640,640]{1,0:T(8,128)(2,1)}, u32[]{:S(2)}, u32[]{:S(2)}) collective-permute-start(bf16[640,640]{1,0:T(8,128)(2,1)S(1)} %collective-permute-done.5.refs_13_), channel_id=1, source_target_pairs={{1,64},{64,1},{65,0},{0,65},{3,66},{66,3},{67,2},{2,67},{5,68},{68... | collective-permute-start | bytes 2457608 | tf_op jit(solution)/shard_map/ppermute | solution.py:26
  38.3 16.3 %collective-permute-done.1.refs_9_ = bf16[640,640]{1,0:T(8,128)(2,1)} collective-permute-done((bf16[640,640]{1,0:T(8,128)(2,1)S(1)}, bf16[640,640]{1,0:T(8,128)(2,1)}, u32[]{:S(2)}, u32[]{:S(2)}) %collective-permute-start.1) | collective-permute-done | bytes 819232 | tf_op jit(solution)/shard_map/ppermute | solution.py:22
  54.6 0.5 collective-permute-start.2
  55.1 0.0 collective-permute-done.3.refs_10_
  55.1 0.4 collective-permute-start.4
  55.5 0.1 collective-permute-start.6
  55.6 0.0 collective-permute-done.7.refs_14_
  55.6 1.8 %collective-permute-start.9 = (bf16[640,640]{1,0:T(8,128)(2,1)}, bf16[640,640]{1,0:T(8,128)(2,1)}, u32[]{:S(2)}, u32[]{:S(2)}) collective-permute-start(bf16[640,640]{1,0:T(8,128)(2,1)} %collective-permute-done.7.refs_14_), channel_id=1, source_target_pairs={{1,64},{64,1},{65,0},{0,65},{3,66},{66,3},{67,2},{2,67},{5,68},{68... | collective-permute-start | bytes 2457608 | tf_op jit(solution)/shard_map/ppermute | solution.py:26
  57.5 1.9 %constant_dynamic-slice_fusion = bf16[640,1920]{1,0:T(8,128)(2,1)S(1)} fusion(bf16[640,5120]{1,0:T(8,128)(2,1)} %refs_8_.1, s32[]{:T(128)S(6)} %select_n.11), kind=kLoop, calls=%fused_computation | loop fusion | bytes 4915204 | tf_op jit(solution)/shard_map/dynamic_slice | solution.py:309
  59.4 0.0 collective-permute-done.8.refs_15_
  59.4 1.5 collective-permute-start.18
  60.9 0.0 collective-permute-done.2.refs_17_
  60.9 1.2 collective-permute-start.19
  62.2 0.6 reshape.14.refs_6_
  62.8 0.6 reshape.15.refs_7_
  63.4 0.7 stack.23.place_ref
  64.1 0.0 collective-permute-done.4.refs_18_
  64.1 0.0 collective-permute-done.6.refs_21_
  64.1 9.2 %all-gather.5.cloned.1.call-done = bf16[32,320,512]{2,1,0:T(8,128)(2,1)} async-done(((bf16[4,320,512]{2,1,0:T(8,128)(2,1)}), bf16[32,320,512]{2,1,0:T(8,128)(2,1)}) %all-gather.5.cloned.1.call-update) | async-done | bytes 10485776 | tf_op jit(solution)/shard_map/all_gather | solution.py:326
  73.3 12.3 %shard_map.123 = bf16[4,336,256]{2,1,0:T(8,128)(2,1)} custom-call(bf16[5,320,256]{2,1,0:T(8,128)(2,1)} %copy-done.9, bf16[8,4,320,512]{3,2,1,0:T(8,128)(2,1)} %bitcast.8), custom_call_target="tpu_custom_call" | custom-call | flops 5033164800 | bytes 1000 | tf_op jit(solution)/shard_map/pallas_call | solution.py:122
  85.6 0.0 collective-permute-done.9.refs_16_
  85.6 0.3 collective-permute-start.10
  85.9 0.3 collective-permute-start.11
  86.1 0.3 collective-permute-start.12
  86.4 1.8 %collective-permute-done.10.refs_22_ = bf16[640,640]{1,0:T(8,128)(2,1)S(1)} collective-permute-done((bf16[640,640]{1,0:T(8,128)(2,1)}, bf16[640,640]{1,0:T(8,128)(2,1)S(1)}, u32[]{:S(2)}, u32[]{:S(2)}) %collective-permute-start.10) | collective-permute-done | bytes 819232 | tf_op jit(solution)/shard_map/ppermute | solution.py:22
  88.2 1.2 collective-permute-start.14
  89.3 12.5 %shard_map.124 = (f32[4,320,256]{2,1,0:T(8,128)}, f32[4,8,320]{2,1,0:T(8,128)}) custom-call(bf16[5,320,256]{2,1,0:T(8,128)(2,1)} %get-tuple-element.33.refs_0_.refs_1_, bf16[8,4,320,512]{3,2,1,0:T(8,128)(2,1)} %bitcast.9), custom_call_target="tpu_custom_call" | custom-call | flops 5033164800 | bytes 1000 | tf_op jit(solution)/shard_map/pallas_call | solution.py:122
  101.8 0.0 collective-permute-done.11.refs_23_
  101.8 0.0 collective-permute-done.12.refs_24_
  101.8 0.0 all-gather.7.cloned.1.call-done
  101.9 7.4 %shard_map.125 = (bf16[1,336,256]{2,1,0:T(8,128)(2,1)}, f32[1,320,256]{2,1,0:T(8,128)}, f32[1,8,320]{2,1,0:T(8,128)}) custom-call(bf16[5,320,256]{2,1,0:T(8,128)(2,1)} %copy-done.9, bf16[5,320,256]{2,1,0:T(8,128)(2,1)} %get-tuple-element.33.refs_0_.refs_1_, bf16[8,1,320,512]{3,2,1,0:T(8,128)(2,1)} %bitcast.10), custom_call_target="tpu_custom_call" | custom-call | flops 2516582400 | bytes 1000 | tf_op jit(solution)/shard_map/pallas_call | solution.py:122
  109.2 0.7 collective-permute-start.13
  110.0 0.0 collective-permute-done.14.far_ref
  110.0 3.6 %shard_map.126 = (bf16[2,80,512]{2,1,0:T(8,128)(2,1)}, bf16[2,80,512]{2,1,0:T(8,128)(2,1)}, bf16[2,80,512]{2,1,0:T(8,128)(2,1)}, bf16[2,80,512]{2,1,0:T(8,128)(2,1)}) custom-call(s32[1]{0:T(128)} %bitcast.5.me_ref, f32[4,320,256]{2,1,0:T(8,128)} %get-tuple-element.44.near_ref, f32[4,8,320]{2,1,0:T(8,128)} %get-tuple-element.34.near_stat, ...), custom_call_target="tpu_custom_call" | custom-call | flops 1000 | bytes 1000 | tf_op jit(solution)/shard_map/pallas_call | solution.py:181
  113.6 1.2 collective-permute-done.18.refs_11_
  114.7 0.0 collective-permute-done.19.refs_12_
  114.7 0.3 collective-permute-done.13.far_ref
  115.0 1.8 %collective-permute-start.20 = (bf16[640,1920]{1,0:T(8,128)(2,1)}, bf16[640,1920]{1,0:T(8,128)(2,1)S(1)}, u32[]{:S(2)}, u32[]{:S(2)}) collective-permute-start(bf16[640,1920]{1,0:T(8,128)(2,1)} %collective-permute-done.18.refs_11_), channel_id=1, source_target_pairs={{0,8},{8,0},{1,9},{9,1},{2,10},{10,2},{3,11},{11,3},{4,12},{12,4},... | collective-permute-start | bytes 7372808 | tf_op jit(solution)/shard_map/ppermute | solution.py:22
  116.8 0.1 collective-permute-start.21
  116.9 2.7 %shard_map.127 = (bf16[2,80,640]{2,1,0:T(8,128)(2,1)}, bf16[2,80,640]{2,1,0:T(8,128)(2,1)}, bf16[2,80,640]{2,1,0:T(8,128)(2,1)}, bf16[2,80,640]{2,1,0:T(8,128)(2,1)}) custom-call(s32[1]{0:T(128)} %bitcast.5.me_ref, f32[1,320,256]{2,1,0:T(8,128)} %get-tuple-element.40.near_ref, f32[1,8,320]{2,1,0:T(8,128)} %get-tuple-element.41.near_stat, ...), custom_call_target="tpu_custom_call" | custom-call | flops 1000 | bytes 1000 | tf_op jit(solution)/shard_map/pallas_call | solution.py:181
  119.5 0.6 collective-permute-start.15
  120.1 2.1 %collective-permute-start.16 = (bf16[2,80,640]{2,1,0:T(8,128)(2,1)}, bf16[2,80,640]{2,1,0:T(8,128)(2,1)S(1)}, u32[]{:S(2)}, u32[]{:S(2)}) collective-permute-start(bf16[2,80,640]{2,1,0:T(8,128)(2,1)} %get-tuple-element.51), channel_id=1, source_target_pairs={{0,6},{2,0},{4,2},{6,4},{1,7},{3,1},{5,3},{7,5},{8,14},{10,8},{12,... | collective-permute-start | bytes 614408 | tf_op jit(solution)/shard_map/ppermute | solution.py:22
  122.2 1.0 collective-permute-start.17
  123.2 3.8 %collective-permute-done.15.refs_1_ = bf16[2,80,640]{2,1,0:T(8,128)(2,1)S(1)} collective-permute-done((bf16[2,80,640]{2,1,0:T(8,128)(2,1)}, bf16[2,80,640]{2,1,0:T(8,128)(2,1)S(1)}, u32[]{:S(2)}, u32[]{:S(2)}) %collective-permute-start.15) | collective-permute-done | bytes 204832 | tf_op jit(solution)/shard_map/ppermute | solution.py:22
  127.0 0.0 collective-permute-done.16.refs_2_
  127.0 5.3 %collective-permute-done.17.refs_3_ = bf16[2,80,640]{2,1,0:T(8,128)(2,1)S(1)} collective-permute-done((bf16[2,80,640]{2,1,0:T(8,128)(2,1)}, bf16[2,80,640]{2,1,0:T(8,128)(2,1)S(1)}, u32[]{:S(2)}, u32[]{:S(2)}) %collective-permute-start.17) | collective-permute-done | bytes 204832 | tf_op jit(solution)/shard_map/ppermute | solution.py:22
  132.4 0.0 collective-permute-done.20.refs_19_
  132.4 0.0 collective-permute-done.21.refs_20_
  132.4 0.6 copy-done.5
  133.0 0.9 copy-done
  133.9 13.3 %shard_map.128 = (bf16[80,5120]{1,0:T(8,128)(2,1)}, bf16[80,5120]{1,0:T(8,128)(2,1)}) custom-call(s32[5]{0:T(128)} %stack.23.place_ref, bf16[2,80,640]{2,1,0:T(8,128)(2,1)} %get-tuple-element.49.refs_0_, bf16[2,80,640]{2,1,0:T(8,128)(2,1)} %copy-done.3, bf16[2,80,640]{2,1,0:T(8,128)(2,1)} %copy-done.4, bf16[2,80,640]{2,1,0:T(8,128)(2,1)} %copy-done.5, ...), custom_call_target="tpu_custom_call" | custom-call | flops 1000 | bytes 1000 | tf_op jit(solution)/shard_map/pallas_call | solution.py:279
  (18 shorter events, 0.0 us)
Async XLA Ops:
  7.2 66.1 %all-gather.5.cloned.1.call-start = ((), (), s32[]{:S(2)}) async-start(), calls=%async_computation | async-start | bytes 11796480 | tf_op jit(solution)/shard_map/all_gather | solution.py:326
  10.7 91.2 %all-gather.7.cloned.1.call-start = ((), (), s32[]{:S(2)}) async-start(), calls=%async_computation.1 | async-start | bytes 2949120 | tf_op jit(solution)/shard_map/all_gather | solution.py:327
  11.5 19.9 %collective-permute-start = (bf16[5,320,256]{2,1,0:T(8,128)(2,1)}, bf16[5,320,256]{2,1,0:T(8,128)(2,1)S(1)}, u32[]{:S(2)}, u32[]{:S(2)}) collective-permute-start(bf16[5,320,256]{2,1,0:T(8,128)(2,1)} %get-tuple-element.33.refs_0_.refs_1_), channel_id=1, source_target_pairs={{0,64},{64,0},{1,65},{65,1},{2,66},{66,2},{3,67},{67,3},{4,68},{68... | collective-permute-start | bytes 2457608 | tf_op jit(solution)/shard_map/ppermute | solution.py:22
  15.2 20.4 %collective-permute-start.5 = (bf16[640,640]{1,0:T(8,128)(2,1)S(1)}, bf16[640,640]{1,0:T(8,128)(2,1)S(1)}, u32[]{:S(2)}, u32[]{:S(2)}) collective-permute-start(bf16[640,640]{1,0:T(8,128)(2,1)S(1)} %get-tuple-element.56), channel_id=1, source_target_pairs={{0,4},{2,6},{4,0},{6,2},{1,5},{3,7},{5,1},{7,3},{8,12},{10,14},{12... | collective-permute-start | bytes 2457608 | tf_op jit(solution)/shard_map/ppermute | solution.py:22
  18.2 36.4 %collective-permute-start.1 = (bf16[640,640]{1,0:T(8,128)(2,1)S(1)}, bf16[640,640]{1,0:T(8,128)(2,1)}, u32[]{:S(2)}, u32[]{:S(2)}) collective-permute-start(bf16[640,640]{1,0:T(8,128)(2,1)S(1)} %get-tuple-element.57), channel_id=1, source_target_pairs={{0,2},{2,4},{4,6},{6,0},{1,3},{3,5},{5,7},{7,1},{8,10},{10,12},{12... | collective-permute-start | bytes 2457608 | tf_op jit(solution)/shard_map/ppermute | solution.py:22
  18.6 36.5 %collective-permute-start.3 = (bf16[640,640]{1,0:T(8,128)(2,1)S(1)}, bf16[640,640]{1,0:T(8,128)(2,1)}, u32[]{:S(2)}, u32[]{:S(2)}) collective-permute-start(bf16[640,640]{1,0:T(8,128)(2,1)S(1)} %get-tuple-element.57), channel_id=1, source_target_pairs={{0,6},{2,0},{4,2},{6,4},{1,7},{3,1},{5,3},{7,5},{8,14},{10,8},{12,... | collective-permute-start | bytes 2457608 | tf_op jit(solution)/shard_map/ppermute | solution.py:22
  31.4 24.3 %copy-start.9 = (bf16[5,320,256]{2,1,0:T(8,128)(2,1)}, bf16[5,320,256]{2,1,0:T(8,128)(2,1)S(1)}, u32[]{:S(2)}) copy-start(bf16[5,320,256]{2,1,0:T(8,128)(2,1)S(1)} %collective-permute-done.refs_0_) | copy-start | bytes 2457604
  35.6 23.8 %copy-start.1 = (bf16[640,640]{1,0:T(8,128)(2,1)}, bf16[640,640]{1,0:T(8,128)(2,1)S(1)}, u32[]{:S(2)}) copy-start(bf16[640,640]{1,0:T(8,128)(2,1)S(1)} %collective-permute-done.5.refs_13_) | copy-start | bytes 2457604
  35.6 20.0 %collective-permute-start.7 = (bf16[640,640]{1,0:T(8,128)(2,1)S(1)}, bf16[640,640]{1,0:T(8,128)(2,1)}, u32[]{:S(2)}, u32[]{:S(2)}) collective-permute-start(bf16[640,640]{1,0:T(8,128)(2,1)S(1)} %collective-permute-done.5.refs_13_), channel_id=1, source_target_pairs={{0,64},{64,0},{1,65},{65,1},{2,66},{66,2},{3,67},{67,3},{4,68},{68... | collective-permute-start | bytes 2457608 | tf_op jit(solution)/shard_map/ppermute | solution.py:22
  35.8 23.6 %collective-permute-start.8 = (bf16[640,640]{1,0:T(8,128)(2,1)S(1)}, bf16[640,640]{1,0:T(8,128)(2,1)}, u32[]{:S(2)}, u32[]{:S(2)}) collective-permute-start(bf16[640,640]{1,0:T(8,128)(2,1)S(1)} %collective-permute-done.5.refs_13_), channel_id=1, source_target_pairs={{1,64},{64,1},{65,0},{0,65},{3,66},{66,3},{67,2},{2,67},{5,68},{68... | collective-permute-start | bytes 2457608 | tf_op jit(solution)/shard_map/ppermute | solution.py:26
  54.6 6.3 %collective-permute-start.2 = (bf16[640,640]{1,0:T(8,128)(2,1)}, bf16[640,640]{1,0:T(8,128)(2,1)}, u32[]{:S(2)}, u32[]{:S(2)}) collective-permute-start(bf16[640,640]{1,0:T(8,128)(2,1)} %collective-permute-done.1.refs_9_), channel_id=1, source_target_pairs={{0,8},{8,0},{1,9},{9,1},{2,10},{10,2},{3,11},{11,3},{4,12},{12,4},... | collective-permute-start | bytes 2457608 | tf_op jit(solution)/shard_map/ppermute | solution.py:22
  55.1 9.0 %collective-permute-start.4 = (bf16[640,640]{1,0:T(8,128)(2,1)}, bf16[640,640]{1,0:T(8,128)(2,1)}, u32[]{:S(2)}, u32[]{:S(2)}) collective-permute-start(bf16[640,640]{1,0:T(8,128)(2,1)} %collective-permute-done.3.refs_10_), channel_id=1, source_target_pairs={{0,8},{8,0},{1,9},{9,1},{2,10},{10,2},{3,11},{11,3},{4,12},{12,4},... | collective-permute-start | bytes 2457608 | tf_op jit(solution)/shard_map/ppermute | solution.py:22
  55.5 8.6 %collective-permute-start.6 = (bf16[640,640]{1,0:T(8,128)(2,1)S(1)}, bf16[640,640]{1,0:T(8,128)(2,1)}, u32[]{:S(2)}, u32[]{:S(2)}) collective-permute-start(bf16[640,640]{1,0:T(8,128)(2,1)S(1)} %collective-permute-done.5.refs_13_), channel_id=1, source_target_pairs={{0,8},{8,0},{1,9},{9,1},{2,10},{10,2},{3,11},{11,3},{4,12},{12,4},... | collective-permute-start | bytes 2457608 | tf_op jit(solution)/shard_map/ppermute | solution.py:22
  55.6 6.6 %copy-start.7 = (bf16[5120]{0:T(1024)(128)(2,1)S(1)}, bf16[5120]{0:T(1024)(128)(2,1)}, u32[]{:S(2)}) copy-start(bf16[5120]{0:T(1024)(128)(2,1)} %param.20) | copy-start | bytes 30724
  55.6 7.2 %copy-start.8 = (bf16[5120]{0:T(1024)(128)(2,1)S(1)}, bf16[5120]{0:T(1024)(128)(2,1)}, u32[]{:S(2)}) copy-start(bf16[5120]{0:T(1024)(128)(2,1)} %param.21) | copy-start | bytes 30724
  55.6 30.0 %collective-permute-start.9 = (bf16[640,640]{1,0:T(8,128)(2,1)}, bf16[640,640]{1,0:T(8,128)(2,1)}, u32[]{:S(2)}, u32[]{:S(2)}) collective-permute-start(bf16[640,640]{1,0:T(8,128)(2,1)} %collective-permute-done.7.refs_14_), channel_id=1, source_target_pairs={{1,64},{64,1},{65,0},{0,65},{3,66},{66,3},{67,2},{2,67},{5,68},{68... | collective-permute-start | bytes 2457608 | tf_op jit(solution)/shard_map/ppermute | solution.py:26
  59.4 55.3 %collective-permute-start.18 = (bf16[640,1920]{1,0:T(8,128)(2,1)S(1)}, bf16[640,1920]{1,0:T(8,128)(2,1)}, u32[]{:S(2)}, u32[]{:S(2)}) collective-permute-start(bf16[640,1920]{1,0:T(8,128)(2,1)S(1)} %constant_dynamic-slice_fusion), channel_id=1, source_target_pairs={{0,2},{2,4},{4,6},{6,0},{1,3},{3,5},{5,7},{7,1},{8,10},{10,12},{12... | collective-permute-start | bytes 7372808 | tf_op jit(solution)/shard_map/ppermute | solution.py:22
  60.9 53.8 %collective-permute-start.19 = (bf16[640,1920]{1,0:T(8,128)(2,1)S(1)}, bf16[640,1920]{1,0:T(8,128)(2,1)}, u32[]{:S(2)}, u32[]{:S(2)}) collective-permute-start(bf16[640,1920]{1,0:T(8,128)(2,1)S(1)} %constant_dynamic-slice_fusion), channel_id=1, source_target_pairs={{0,6},{2,0},{4,2},{6,4},{1,7},{3,1},{5,3},{7,5},{8,14},{10,8},{12,... | collective-permute-start | bytes 7372808 | tf_op jit(solution)/shard_map/ppermute | solution.py:22
  85.6 2.5 %collective-permute-start.10 = (bf16[640,640]{1,0:T(8,128)(2,1)}, bf16[640,640]{1,0:T(8,128)(2,1)S(1)}, u32[]{:S(2)}, u32[]{:S(2)}) collective-permute-start(bf16[640,640]{1,0:T(8,128)(2,1)} %collective-permute-done.7.refs_14_), channel_id=1, source_target_pairs={{0,8},{8,0},{1,9},{9,1},{2,10},{10,2},{3,11},{11,3},{4,12},{12,4},... | collective-permute-start | bytes 2457608 | tf_op jit(solution)/shard_map/ppermute | solution.py:22
  85.9 16.0 %collective-permute-start.11 = (bf16[640,640]{1,0:T(8,128)(2,1)}, bf16[640,640]{1,0:T(8,128)(2,1)}, u32[]{:S(2)}, u32[]{:S(2)}) collective-permute-start(bf16[640,640]{1,0:T(8,128)(2,1)} %collective-permute-done.8.refs_15_), channel_id=1, source_target_pairs={{0,8},{8,0},{1,9},{9,1},{2,10},{10,2},{3,11},{11,3},{4,12},{12,4},... | collective-permute-start | bytes 2457608 | tf_op jit(solution)/shard_map/ppermute | solution.py:22
  86.1 15.7 %collective-permute-start.12 = (bf16[640,640]{1,0:T(8,128)(2,1)}, bf16[640,640]{1,0:T(8,128)(2,1)}, u32[]{:S(2)}, u32[]{:S(2)}) collective-permute-start(bf16[640,640]{1,0:T(8,128)(2,1)} %collective-permute-done.9.refs_16_), channel_id=1, source_target_pairs={{0,8},{8,0},{1,9},{9,1},{2,10},{10,2},{3,11},{11,3},{4,12},{12,4},... | collective-permute-start | bytes 2457608 | tf_op jit(solution)/shard_map/ppermute | solution.py:22
  88.1 13.7 %copy-start.2 = (bf16[640,640]{1,0:T(8,128)(2,1)}, bf16[640,640]{1,0:T(8,128)(2,1)S(1)}, u32[]{:S(2)}) copy-start(bf16[640,640]{1,0:T(8,128)(2,1)S(1)} %collective-permute-done.10.refs_22_) | copy-start | bytes 2457604
  88.2 21.8 %collective-permute-start.14 = (bf16[4,336,256]{2,1,0:T(8,128)(2,1)}, bf16[4,336,256]{2,1,0:T(8,128)(2,1)}, u32[]{:S(2)}, u32[]{:S(2)}) collective-permute-start(bf16[4,336,256]{2,1,0:T(8,128)(2,1)} %shard_map.123), channel_id=1, source_target_pairs={{0,64},{64,0},{1,65},{65,1},{2,66},{66,2},{3,67},{67,3},{4,68},{68... | collective-permute-start | bytes 2064392 | tf_op jit(solution)/shard_map/ppermute | solution.py:22
  109.2 5.7 %collective-permute-start.13 = (bf16[1,336,256]{2,1,0:T(8,128)(2,1)}, bf16[1,336,256]{2,1,0:T(8,128)(2,1)S(1)}, u32[]{:S(2)}, u32[]{:S(2)}) collective-permute-start(bf16[1,336,256]{2,1,0:T(8,128)(2,1)} %get-tuple-element.42), channel_id=1, source_target_pairs={{0,64},{64,0},{1,65},{65,1},{2,66},{66,2},{3,67},{67,3},{4,68},{68... | collective-permute-start | bytes 516104 | tf_op jit(solution)/shard_map/ppermute | solution.py:22
  115.0 1.9 %copy-start.6 = (bf16[1,336,256]{2,1,0:T(8,128)(2,1)}, bf16[1,336,256]{2,1,0:T(8,128)(2,1)S(1)}, u32[]{:S(2)}) copy-start(bf16[1,336,256]{2,1,0:T(8,128)(2,1)S(1)} %collective-permute-done.13.far_ref) | copy-start | bytes 516100
  115.0 17.4 %collective-permute-start.20 = (bf16[640,1920]{1,0:T(8,128)(2,1)}, bf16[640,1920]{1,0:T(8,128)(2,1)S(1)}, u32[]{:S(2)}, u32[]{:S(2)}) collective-permute-start(bf16[640,1920]{1,0:T(8,128)(2,1)} %collective-permute-done.18.refs_11_), channel_id=1, source_target_pairs={{0,8},{8,0},{1,9},{9,1},{2,10},{10,2},{3,11},{11,3},{4,12},{12,4},... | collective-permute-start | bytes 7372808 | tf_op jit(solution)/shard_map/ppermute | solution.py:22
  116.8 15.6 %collective-permute-start.21 = (bf16[640,1920]{1,0:T(8,128)(2,1)}, bf16[640,1920]{1,0:T(8,128)(2,1)}, u32[]{:S(2)}, u32[]{:S(2)}) collective-permute-start(bf16[640,1920]{1,0:T(8,128)(2,1)} %collective-permute-done.19.refs_12_), channel_id=1, source_target_pairs={{0,8},{8,0},{1,9},{9,1},{2,10},{10,2},{3,11},{11,3},{4,12},{12,4},... | collective-permute-start | bytes 7372808 | tf_op jit(solution)/shard_map/ppermute | solution.py:22
  119.5 7.5 %collective-permute-start.15 = (bf16[2,80,640]{2,1,0:T(8,128)(2,1)}, bf16[2,80,640]{2,1,0:T(8,128)(2,1)S(1)}, u32[]{:S(2)}, u32[]{:S(2)}) collective-permute-start(bf16[2,80,640]{2,1,0:T(8,128)(2,1)} %get-tuple-element.50), channel_id=1, source_target_pairs={{0,2},{2,4},{4,6},{6,0},{1,3},{3,5},{5,7},{7,1},{8,10},{10,12},{12... | collective-permute-start | bytes 614408 | tf_op jit(solution)/shard_map/ppermute | solution.py:22
  120.1 6.9 %collective-permute-start.16 = (bf16[2,80,640]{2,1,0:T(8,128)(2,1)}, bf16[2,80,640]{2,1,0:T(8,128)(2,1)S(1)}, u32[]{:S(2)}, u32[]{:S(2)}) collective-permute-start(bf16[2,80,640]{2,1,0:T(8,128)(2,1)} %get-tuple-element.51), channel_id=1, source_target_pairs={{0,6},{2,0},{4,2},{6,4},{1,7},{3,1},{5,3},{7,5},{8,14},{10,8},{12,... | collective-permute-start | bytes 614408 | tf_op jit(solution)/shard_map/ppermute | solution.py:22
  122.2 10.1 %collective-permute-start.17 = (bf16[2,80,640]{2,1,0:T(8,128)(2,1)}, bf16[2,80,640]{2,1,0:T(8,128)(2,1)S(1)}, u32[]{:S(2)}, u32[]{:S(2)}) collective-permute-start(bf16[2,80,640]{2,1,0:T(8,128)(2,1)} %get-tuple-element.52), channel_id=1, source_target_pairs={{0,4},{2,6},{4,0},{6,2},{1,5},{3,7},{5,1},{7,3},{8,12},{10,14},{12... | collective-permute-start | bytes 614408 | tf_op jit(solution)/shard_map/ppermute | solution.py:22
  127.0 5.4 %copy-start.3 = (bf16[2,80,640]{2,1,0:T(8,128)(2,1)}, bf16[2,80,640]{2,1,0:T(8,128)(2,1)S(1)}, u32[]{:S(2)}) copy-start(bf16[2,80,640]{2,1,0:T(8,128)(2,1)S(1)} %collective-permute-done.15.refs_1_) | copy-start | bytes 614404
  127.0 5.4 %copy-start.4 = (bf16[2,80,640]{2,1,0:T(8,128)(2,1)}, bf16[2,80,640]{2,1,0:T(8,128)(2,1)S(1)}, u32[]{:S(2)}) copy-start(bf16[2,80,640]{2,1,0:T(8,128)(2,1)S(1)} %collective-permute-done.16.refs_2_) | copy-start | bytes 614404
  132.4 0.7 copy-start.5
  132.4 1.5 %copy-start = (bf16[640,1920]{1,0:T(8,128)(2,1)}, bf16[640,1920]{1,0:T(8,128)(2,1)S(1)}, u32[]{:S(2)}) copy-start(bf16[640,1920]{1,0:T(8,128)(2,1)S(1)} %collective-permute-done.20.refs_19_) | copy-start | bytes 7372804
Sparse Core Ops, SparseCore 0:
  10.8 62.3 all-gather.4
  74.9 26.4 all-gather.6

commit v2 on v1

--- a/solution.py
+++ b/solution.py
@@ -220,10 +220,10 @@
 
 def project_kernel(parts, place_ref, *refs):
     atts, refs = refs[:parts], refs[parts:]
-    stream, t_stream, gate, t_gate, weight = refs[:5]
+    gate, t_gate, stream_in, t_stream_in, weight = refs[:5]
     pieces = refs[5:21]
-    result, t_result, att, narrow, broad, sems = refs[21:]
-    rows = stream.shape[0]
+    result, t_result, att, streams, narrow, broad, stream_sems, sems = refs[21:]
+    rows = stream_in.shape[0]
     depth = weight.shape[0]
     core = place_ref[0]
     steps = []
@@ -251,13 +251,21 @@
 
                 group.append(pltpu.make_async_copy(far[0], to, sem.at[3 + j]))
             steps.append((slot, col, count * WIDE, group))
+    moves = [
+        pltpu.make_async_copy(source, streams.at[i], stream_sems.at[i])
+        for i, source in enumerate((stream_in, t_stream_in))
+    ]
+    for move in moves:
+        move.start()
     at = 0
     for ref in atts:
         size = ref.shape[2]
         att[:rows, at : at + size] = ref[0]
         att[rows:, at : at + size] = ref[1]
         at += size
-    for slot, col, width, group in steps:
+    for i, (slot, col, width, group) in enumerate(steps):
+        if i == 0:
+            group = group + moves
         for move in group:
             move.wait()
         sums = jnp.dot(att[...], slot[...], preferred_element_type=jnp.float32)
@@ -265,9 +273,9 @@
         cols = pl.ds(col, width)
         g = gate[:, cols].astype(jnp.float32)
         tg = t_gate[:, cols].astype(jnp.float32)
-        result[:, cols] = (stream[:, cols].astype(jnp.float32) + g * branch).astype(result.dtype)
+        result[:, cols] = (streams[0, :, cols].astype(jnp.float32) + g * branch).astype(result.dtype)
         t_result[:, cols] = (
-            t_stream[:, cols].astype(jnp.float32) + tg * branch + g * t_branch
+            streams[1, :, cols].astype(jnp.float32) + tg * branch + g * t_branch
         ).astype(t_result.dtype)
 
 
@@ -279,19 +287,21 @@
     return pl.pallas_call(
         functools.partial(project_kernel, len(atts)),
         in_specs=[pl.BlockSpec(memory_space=pltpu.SMEM)]
-        + [whole] * (len(atts) + 4)
-        + [away] * (1 + len(pieces)),
+        + [whole] * (len(atts) + 2)
+        + [away] * (3 + len(pieces)),
         out_specs=[whole] * 2,
         out_shape=[jax.ShapeDtypeStruct((rows, columns), stream.dtype)] * 2,
         scratch_shapes=[
             pltpu.VMEM((2 * rows, 4 * depth), jnp.bfloat16),
+            pltpu.VMEM((2, rows, columns), jnp.bfloat16),
             pltpu.VMEM((2, 4 * depth, WIDE), jnp.bfloat16),
             pltpu.VMEM((2, 4 * depth, 3 * WIDE), jnp.bfloat16),
+            pltpu.SemaphoreType.DMA((2,)),
             pltpu.SemaphoreType.DMA((4, 6)),
         ],
         compiler_params=pltpu.CompilerParams(vmem_limit_bytes=VMEM),
         cost_estimate=pl.CostEstimate(flops=1000, bytes_accessed=1000, transcendentals=0),
-    )(place, *atts, stream, t_stream, gate, t_gate, weight, *pieces)
+    )(place, *atts, gate, t_gate, stream, t_stream, weight, *pieces)
 
 
 def on_device(

time: 154 us -> 158 us (1.026)
  Pallas kernels: 55.2 us -> 58.9 us
    pallas_call x1, Pallas kernels: 13.3 us -> 17 us  [project(): pl.pallas_call(functools.partial(project_kernel, len(atts)), in_specs=[pl...]
  transfers between devices with their start and end apart: 24 -> 24, of which waited for: 9 -> 9; matrix products, arithmetic and copies ran while one was open for 4% -> 3% of each run, Pallas kernels for 25% -> 24%
where the time goes in v2:
time: 158 us
  Pallas kernels  58.9 us (37%)
  waiting for transfers between devices  53.4 us (34%)
  starting transfers between devices  24.4 us (15%)
  between operations  14.2 us (9%)
  local copies, waits for them, and re-layouts  6.98 us (4%)
    ppermute x20, waiting for transfers between devices, shift(): lax.ppermute(value, axis, [(i, (i + step) % size) for i in range(size)])  43.5 us
    pallas_call x3, Pallas kernels, attend(): pl.pallas_call(functools.partial(attend_kernel, sent), grid=(heads,), in_...  32.2 us
    ppermute x20, starting transfers between devices, shift(): lax.ppermute(value, axis, [(i, (i + step) % size) for i in range(size)])  20 us
    pallas_call x1, Pallas kernels, project(): pl.pallas_call(functools.partial(project_kernel, len(atts)), in_specs=[pl...  17 us
    all_gather x1, waiting for transfers between devices, on_device(): kv_a = lax.all_gather(lot_a, ('z', 'core'))  9.19 us
    pallas_call x2, Pallas kernels, merge(): pl.pallas_call(merge_kernel, in_specs=[pl.BlockSpec(memory_space=pltpu.SM...  6.22 us
    ppermute x2, starting transfers between devices, swap_parts(): return lax.ppermute(value, ('xl', 'dp'), [(1, 2), (2, 1), (3, 0), (0, 3)])  4.32 us
    dynamic_slice x2, local copies, waits for them, and re-layouts, quarter(): lax.dynamic_slice(out_weight, (0, core * half_width + place * WIDE), (dep...  3.54 us
  transfers between devices with their start and end apart: 24, of which 9 were waited for; matrix products, arithmetic and copies ran while one was open for 3% of the time, Pallas kernels for 24%

profile of v2, /device:TPU:1, one launch (start us, length us, event | category | flops | bytes accessed | tf_op | source)
XLA Modules:
  0.0 157.8 jit_solution(3388772969074700080)
XLA Ops:
  7.2 0.0 all-gather.5.cloned.1.call-start
  7.2 3.5 %shard_map.122 = (bf16[4,320,512]{2,1,0:T(8,128)(2,1)}, bf16[1,320,512]{2,1,0:T(8,128)(2,1)}, bf16[5,320,256]{2,1,0:T(8,128)(2,1)}) custom-call(bf16[320,640]{1,0:T(8,128)(2,1)} %q.1, bf16[320,640]{1,0:T(8,128)(2,1)} %t_q.1, bf16[320,640]{1,0:T(8,128)(2,1)} %k.1, bf16[320,640]{1,0:T(8,128)(2,1)} %t_k.1, bf16[320,640]{1,0:T(8,128)(2,1)} %v.1, ...), custom_call_target="tpu_custom_call" | custom-call | flops 1000 | bytes 1000 | tf_op jit(solution)/shard_map/pallas_call | solution.py:207
  10.7 0.0 all-gather.5.cloned.1.call-update
  10.7 0.0 all-gather.7.cloned.1.call-start
  10.8 0.7 all-gather.7.cloned.1.call-update
  11.5 2.1 %collective-permute-start = (bf16[5,320,256]{2,1,0:T(8,128)(2,1)}, bf16[5,320,256]{2,1,0:T(8,128)(2,1)S(1)}, u32[]{:S(2)}, u32[]{:S(2)}) collective-permute-start(bf16[5,320,256]{2,1,0:T(8,128)(2,1)} %get-tuple-element.33.refs_0_.refs_1_), channel_id=1, source_target_pairs={{0,64},{64,0},{1,65},{65,1},{2,66},{66,2},{3,67},{67,3},{4,68},{68... | collective-permute-start | bytes 2457608 | tf_op jit(solution)/shard_map/ppermute | solution.py:22
  13.6 1.6 %constant_dynamic-slice_fusion.1 = (bf16[640,640]{1,0:T(8,128)(2,1)S(1)}, bf16[640,640]{1,0:T(8,128)(2,1)S(1)}) fusion(bf16[640,5120]{1,0:T(8,128)(2,1)} %refs_8_.1, s32[]{:T(128)S(6)} %select_n.10, s32[]{:T(128)S(6)} %select_n.9), kind=kLoop, calls=%fused_computation.1 | loop fusion | bytes 3276808 | tf_op jit(solution)/shard_map/dynamic_slice | solution.py:319
  15.2 3.0 %collective-permute-start.5 = (bf16[640,640]{1,0:T(8,128)(2,1)S(1)}, bf16[640,640]{1,0:T(8,128)(2,1)S(1)}, u32[]{:S(2)}, u32[]{:S(2)}) collective-permute-start(bf16[640,640]{1,0:T(8,128)(2,1)S(1)} %get-tuple-element.56), channel_id=1, source_target_pairs={{0,4},{2,6},{4,0},{6,2},{1,5},{3,7},{5,1},{7,3},{8,12},{10,14},{12... | collective-permute-start | bytes 2457608 | tf_op jit(solution)/shard_map/ppermute | solution.py:22
  18.2 0.4 collective-permute-start.1
  18.6 2.3 %collective-permute-start.3 = (bf16[640,640]{1,0:T(8,128)(2,1)S(1)}, bf16[640,640]{1,0:T(8,128)(2,1)}, u32[]{:S(2)}, u32[]{:S(2)}) collective-permute-start(bf16[640,640]{1,0:T(8,128)(2,1)S(1)} %get-tuple-element.57), channel_id=1, source_target_pairs={{0,6},{2,0},{4,2},{6,4},{1,7},{3,1},{5,3},{7,5},{8,14},{10,8},{12,... | collective-permute-start | bytes 2457608 | tf_op jit(solution)/shard_map/ppermute | solution.py:22
  20.9 10.5 %collective-permute-done.refs_0_ = bf16[5,320,256]{2,1,0:T(8,128)(2,1)S(1)} collective-permute-done((bf16[5,320,256]{2,1,0:T(8,128)(2,1)}, bf16[5,320,256]{2,1,0:T(8,128)(2,1)S(1)}, u32[]{:S(2)}, u32[]{:S(2)}) %collective-permute-start) | collective-permute-done | bytes 819232 | tf_op jit(solution)/shard_map/ppermute | solution.py:22
  31.4 4.3 %collective-permute-done.5.refs_13_ = bf16[640,640]{1,0:T(8,128)(2,1)S(1)} collective-permute-done((bf16[640,640]{1,0:T(8,128)(2,1)S(1)}, bf16[640,640]{1,0:T(8,128)(2,1)S(1)}, u32[]{:S(2)}, u32[]{:S(2)}) %collective-permute-start.5) | collective-permute-done | bytes 819232 | tf_op jit(solution)/shard_map/ppermute | solution.py:22
  35.6 0.2 collective-permute-start.7
  35.8 2.5 %collective-permute-start.8 = (bf16[640,640]{1,0:T(8,128)(2,1)S(1)}, bf16[640,640]{1,0:T(8,128)(2,1)}, u32[]{:S(2)}, u32[]{:S(2)}) collective-permute-start(bf16[640,640]{1,0:T(8,128)(2,1)S(1)} %collective-permute-done.5.refs_13_), channel_id=1, source_target_pairs={{1,64},{64,1},{65,0},{0,65},{3,66},{66,3},{67,2},{2,67},{5,68},{68... | collective-permute-start | bytes 2457608 | tf_op jit(solution)/shard_map/ppermute | solution.py:26
  38.3 16.3 %collective-permute-done.1.refs_9_ = bf16[640,640]{1,0:T(8,128)(2,1)} collective-permute-done((bf16[640,640]{1,0:T(8,128)(2,1)S(1)}, bf16[640,640]{1,0:T(8,128)(2,1)}, u32[]{:S(2)}, u32[]{:S(2)}) %collective-permute-start.1) | collective-permute-done | bytes 819232 | tf_op jit(solution)/shard_map/ppermute | solution.py:22
  54.6 0.5 collective-permute-start.2
  55.1 0.0 collective-permute-done.3.refs_10_
  55.1 0.4 collective-permute-start.4
  55.5 0.1 collective-permute-start.6
  55.6 0.0 collective-permute-done.7.refs_14_
  55.6 1.8 %collective-permute-start.9 = (bf16[640,640]{1,0:T(8,128)(2,1)}, bf16[640,640]{1,0:T(8,128)(2,1)}, u32[]{:S(2)}, u32[]{:S(2)}) collective-permute-start(bf16[640,640]{1,0:T(8,128)(2,1)} %collective-permute-done.7.refs_14_), channel_id=1, source_target_pairs={{1,64},{64,1},{65,0},{0,65},{3,66},{66,3},{67,2},{2,67},{5,68},{68... | collective-permute-start | bytes 2457608 | tf_op jit(solution)/shard_map/ppermute | solution.py:26
  57.5 1.9 %constant_dynamic-slice_fusion = bf16[640,1920]{1,0:T(8,128)(2,1)S(1)} fusion(bf16[640,5120]{1,0:T(8,128)(2,1)} %refs_8_.1, s32[]{:T(128)S(6)} %select_n.11), kind=kLoop, calls=%fused_computation | loop fusion | bytes 4915204 | tf_op jit(solution)/shard_map/dynamic_slice | solution.py:319
  59.4 0.0 collective-permute-done.8.refs_15_
  59.4 1.5 collective-permute-start.18
  60.9 0.0 collective-permute-done.2.refs_17_
  60.9 1.2 collective-permute-start.19
  62.2 0.6 reshape.14.refs_4_
  62.8 0.6 reshape.15.refs_5_
  63.4 0.7 stack.23.place_ref
  64.1 0.0 collective-permute-done.4.refs_18_
  64.1 0.0 collective-permute-done.6.refs_21_
  64.1 9.2 %all-gather.5.cloned.1.call-done = bf16[32,320,512]{2,1,0:T(8,128)(2,1)} async-done(((bf16[4,320,512]{2,1,0:T(8,128)(2,1)}), bf16[32,320,512]{2,1,0:T(8,128)(2,1)}) %all-gather.5.cloned.1.call-update) | async-done | bytes 10485776 | tf_op jit(solution)/shard_map/all_gather | solution.py:336
  73.3 12.3 %shard_map.123 = bf16[4,336,256]{2,1,0:T(8,128)(2,1)} custom-call(bf16[5,320,256]{2,1,0:T(8,128)(2,1)} %copy-done.9, bf16[8,4,320,512]{3,2,1,0:T(8,128)(2,1)} %bitcast.8), custom_call_target="tpu_custom_call" | custom-call | flops 5033164800 | bytes 1000 | tf_op jit(solution)/shard_map/pallas_call | solution.py:122
  85.6 0.0 collective-permute-done.9.refs_16_
  85.6 0.3 collective-permute-start.10
  85.9 0.3 collective-permute-start.11
  86.1 0.3 collective-permute-start.12
  86.4 1.8 %collective-permute-done.10.refs_22_ = bf16[640,640]{1,0:T(8,128)(2,1)S(1)} collective-permute-done((bf16[640,640]{1,0:T(8,128)(2,1)}, bf16[640,640]{1,0:T(8,128)(2,1)S(1)}, u32[]{:S(2)}, u32[]{:S(2)}) %collective-permute-start.10) | collective-permute-done | bytes 819232 | tf_op jit(solution)/shard_map/ppermute | solution.py:22
  88.2 1.2 collective-permute-start.14
  89.3 12.5 %shard_map.124 = (f32[4,320,256]{2,1,0:T(8,128)}, f32[4,8,320]{2,1,0:T(8,128)}) custom-call(bf16[5,320,256]{2,1,0:T(8,128)(2,1)} %get-tuple-element.33.refs_0_.refs_1_, bf16[8,4,320,512]{3,2,1,0:T(8,128)(2,1)} %bitcast.9), custom_call_target="tpu_custom_call" | custom-call | flops 5033164800 | bytes 1000 | tf_op jit(solution)/shard_map/pallas_call | solution.py:122
  101.8 0.0 collective-permute-done.11.refs_23_
  101.8 0.0 collective-permute-done.12.refs_24_
  101.8 0.0 all-gather.7.cloned.1.call-done
  101.9 7.4 %shard_map.125 = (bf16[1,336,256]{2,1,0:T(8,128)(2,1)}, f32[1,320,256]{2,1,0:T(8,128)}, f32[1,8,320]{2,1,0:T(8,128)}) custom-call(bf16[5,320,256]{2,1,0:T(8,128)(2,1)} %copy-done.9, bf16[5,320,256]{2,1,0:T(8,128)(2,1)} %get-tuple-element.33.refs_0_.refs_1_, bf16[8,1,320,512]{3,2,1,0:T(8,128)(2,1)} %bitcast.10), custom_call_target="tpu_custom_call" | custom-call | flops 2516582400 | bytes 1000 | tf_op jit(solution)/shard_map/pallas_call | solution.py:122
  109.2 0.7 collective-permute-start.13
  110.0 0.0 collective-permute-done.14.far_ref
  110.0 3.6 %shard_map.126 = (bf16[2,80,512]{2,1,0:T(8,128)(2,1)}, bf16[2,80,512]{2,1,0:T(8,128)(2,1)}, bf16[2,80,512]{2,1,0:T(8,128)(2,1)}, bf16[2,80,512]{2,1,0:T(8,128)(2,1)}) custom-call(s32[1]{0:T(128)} %bitcast.5.me_ref, f32[4,320,256]{2,1,0:T(8,128)} %get-tuple-element.44.near_ref, f32[4,8,320]{2,1,0:T(8,128)} %get-tuple-element.34.near_stat, ...), custom_call_target="tpu_custom_call" | custom-call | flops 1000 | bytes 1000 | tf_op jit(solution)/shard_map/pallas_call | solution.py:181
  113.6 1.2 collective-permute-done.18.refs_11_
  114.7 0.0 collective-permute-done.19.refs_12_
  114.7 0.3 collective-permute-done.13.far_ref
  115.0 1.8 %collective-permute-start.20 = (bf16[640,1920]{1,0:T(8,128)(2,1)}, bf16[640,1920]{1,0:T(8,128)(2,1)S(1)}, u32[]{:S(2)}, u32[]{:S(2)}) collective-permute-start(bf16[640,1920]{1,0:T(8,128)(2,1)} %collective-permute-done.18.refs_11_), channel_id=1, source_target_pairs={{0,8},{8,0},{1,9},{9,1},{2,10},{10,2},{3,11},{11,3},{4,12},{12,4},... | collective-permute-start | bytes 7372808 | tf_op jit(solution)/shard_map/ppermute | solution.py:22
  116.8 0.1 collective-permute-start.21
  116.9 2.7 %shard_map.127 = (bf16[2,80,640]{2,1,0:T(8,128)(2,1)}, bf16[2,80,640]{2,1,0:T(8,128)(2,1)}, bf16[2,80,640]{2,1,0:T(8,128)(2,1)}, bf16[2,80,640]{2,1,0:T(8,128)(2,1)}) custom-call(s32[1]{0:T(128)} %bitcast.5.me_ref, f32[1,320,256]{2,1,0:T(8,128)} %get-tuple-element.40.near_ref, f32[1,8,320]{2,1,0:T(8,128)} %get-tuple-element.41.near_stat, ...), custom_call_target="tpu_custom_call" | custom-call | flops 1000 | bytes 1000 | tf_op jit(solution)/shard_map/pallas_call | solution.py:181
  119.5 0.6 collective-permute-start.15
  120.1 2.1 %collective-permute-start.16 = (bf16[2,80,640]{2,1,0:T(8,128)(2,1)}, bf16[2,80,640]{2,1,0:T(8,128)(2,1)S(1)}, u32[]{:S(2)}, u32[]{:S(2)}) collective-permute-start(bf16[2,80,640]{2,1,0:T(8,128)(2,1)} %get-tuple-element.51), channel_id=1, source_target_pairs={{0,6},{2,0},{4,2},{6,4},{1,7},{3,1},{5,3},{7,5},{8,14},{10,8},{12,... | collective-permute-start | bytes 614408 | tf_op jit(solution)/shard_map/ppermute | solution.py:22
  122.2 1.0 collective-permute-start.17
  123.2 3.8 %collective-permute-done.15.refs_1_ = bf16[2,80,640]{2,1,0:T(8,128)(2,1)S(1)} collective-permute-done((bf16[2,80,640]{2,1,0:T(8,128)(2,1)}, bf16[2,80,640]{2,1,0:T(8,128)(2,1)S(1)}, u32[]{:S(2)}, u32[]{:S(2)}) %collective-permute-start.15) | collective-permute-done | bytes 204832 | tf_op jit(solution)/shard_map/ppermute | solution.py:22
  127.0 0.0 collective-permute-done.16.refs_2_
  127.0 5.3 %collective-permute-done.17.refs_3_ = bf16[2,80,640]{2,1,0:T(8,128)(2,1)S(1)} collective-permute-done((bf16[2,80,640]{2,1,0:T(8,128)(2,1)}, bf16[2,80,640]{2,1,0:T(8,128)(2,1)S(1)}, u32[]{:S(2)}, u32[]{:S(2)}) %collective-permute-start.17) | collective-permute-done | bytes 204832 | tf_op jit(solution)/shard_map/ppermute | solution.py:22
  132.4 0.0 collective-permute-done.20.refs_19_
  132.4 0.0 collective-permute-done.21.refs_20_
  132.4 0.6 copy-done.5
  133.0 0.9 copy-done
  133.9 17.0 %shard_map.128 = (bf16[80,5120]{1,0:T(8,128)(2,1)}, bf16[80,5120]{1,0:T(8,128)(2,1)}) custom-call(s32[5]{0:T(128)} %stack.23.place_ref, bf16[2,80,640]{2,1,0:T(8,128)(2,1)} %get-tuple-element.49.refs_0_, bf16[2,80,640]{2,1,0:T(8,128)(2,1)} %copy-done.3, bf16[2,80,640]{2,1,0:T(8,128)(2,1)} %copy-done.4, bf16[2,80,640]{2,1,0:T(8,128)(2,1)} %copy-done.5, ...), custom_call_target="tpu_custom_call" | custom-call | flops 1000 | bytes 1000 | tf_op jit(solution)/shard_map/pallas_call | solution.py:287
  (18 shorter events, 0.0 us)
Async XLA Ops:
  7.2 66.1 %all-gather.5.cloned.1.call-start = ((), (), s32[]{:S(2)}) async-start(), calls=%async_computation | async-start | bytes 11796480 | tf_op jit(solution)/shard_map/all_gather | solution.py:336
  10.7 91.2 %all-gather.7.cloned.1.call-start = ((), (), s32[]{:S(2)}) async-start(), calls=%async_computation.1 | async-start | bytes 2949120 | tf_op jit(solution)/shard_map/all_gather | solution.py:337
  11.5 19.9 %collective-permute-start = (bf16[5,320,256]{2,1,0:T(8,128)(2,1)}, bf16[5,320,256]{2,1,0:T(8,128)(2,1)S(1)}, u32[]{:S(2)}, u32[]{:S(2)}) collective-permute-start(bf16[5,320,256]{2,1,0:T(8,128)(2,1)} %get-tuple-element.33.refs_0_.refs_1_), channel_id=1, source_target_pairs={{0,64},{64,0},{1,65},{65,1},{2,66},{66,2},{3,67},{67,3},{4,68},{68... | collective-permute-start | bytes 2457608 | tf_op jit(solution)/shard_map/ppermute | solution.py:22
  15.2 20.4 %collective-permute-start.5 = (bf16[640,640]{1,0:T(8,128)(2,1)S(1)}, bf16[640,640]{1,0:T(8,128)(2,1)S(1)}, u32[]{:S(2)}, u32[]{:S(2)}) collective-permute-start(bf16[640,640]{1,0:T(8,128)(2,1)S(1)} %get-tuple-element.56), channel_id=1, source_target_pairs={{0,4},{2,6},{4,0},{6,2},{1,5},{3,7},{5,1},{7,3},{8,12},{10,14},{12... | collective-permute-start | bytes 2457608 | tf_op jit(solution)/shard_map/ppermute | solution.py:22
  18.2 36.4 %collective-permute-start.1 = (bf16[640,640]{1,0:T(8,128)(2,1)S(1)}, bf16[640,640]{1,0:T(8,128)(2,1)}, u32[]{:S(2)}, u32[]{:S(2)}) collective-permute-start(bf16[640,640]{1,0:T(8,128)(2,1)S(1)} %get-tuple-element.57), channel_id=1, source_target_pairs={{0,2},{2,4},{4,6},{6,0},{1,3},{3,5},{5,7},{7,1},{8,10},{10,12},{12... | collective-permute-start | bytes 2457608 | tf_op jit(solution)/shard_map/ppermute | solution.py:22
  18.6 36.5 %collective-permute-start.3 = (bf16[640,640]{1,0:T(8,128)(2,1)S(1)}, bf16[640,640]{1,0:T(8,128)(2,1)}, u32[]{:S(2)}, u32[]{:S(2)}) collective-permute-start(bf16[640,640]{1,0:T(8,128)(2,1)S(1)} %get-tuple-element.57), channel_id=1, source_target_pairs={{0,6},{2,0},{4,2},{6,4},{1,7},{3,1},{5,3},{7,5},{8,14},{10,8},{12,... | collective-permute-start | bytes 2457608 | tf_op jit(solution)/shard_map/ppermute | solution.py:22
  31.4 24.3 %copy-start.9 = (bf16[5,320,256]{2,1,0:T(8,128)(2,1)}, bf16[5,320,256]{2,1,0:T(8,128)(2,1)S(1)}, u32[]{:S(2)}) copy-start(bf16[5,320,256]{2,1,0:T(8,128)(2,1)S(1)} %collective-permute-done.refs_0_) | copy-start | bytes 2457604
  35.6 23.8 %copy-start.1 = (bf16[640,640]{1,0:T(8,128)(2,1)}, bf16[640,640]{1,0:T(8,128)(2,1)S(1)}, u32[]{:S(2)}) copy-start(bf16[640,640]{1,0:T(8,128)(2,1)S(1)} %collective-permute-done.5.refs_13_) | copy-start | bytes 2457604
  35.6 20.0 %collective-permute-start.7 = (bf16[640,640]{1,0:T(8,128)(2,1)S(1)}, bf16[640,640]{1,0:T(8,128)(2,1)}, u32[]{:S(2)}, u32[]{:S(2)}) collective-permute-start(bf16[640,640]{1,0:T(8,128)(2,1)S(1)} %collective-permute-done.5.refs_13_), channel_id=1, source_target_pairs={{0,64},{64,0},{1,65},{65,1},{2,66},{66,2},{3,67},{67,3},{4,68},{68... | collective-permute-start | bytes 2457608 | tf_op jit(solution)/shard_map/ppermute | solution.py:22
  35.8 23.6 %collective-permute-start.8 = (bf16[640,640]{1,0:T(8,128)(2,1)S(1)}, bf16[640,640]{1,0:T(8,128)(2,1)}, u32[]{:S(2)}, u32[]{:S(2)}) collective-permute-start(bf16[640,640]{1,0:T(8,128)(2,1)S(1)} %collective-permute-done.5.refs_13_), channel_id=1, source_target_pairs={{1,64},{64,1},{65,0},{0,65},{3,66},{66,3},{67,2},{2,67},{5,68},{68... | collective-permute-start | bytes 2457608 | tf_op jit(solution)/shard_map/ppermute | solution.py:26
  54.6 6.3 %collective-permute-start.2 = (bf16[640,640]{1,0:T(8,128)(2,1)}, bf16[640,640]{1,0:T(8,128)(2,1)}, u32[]{:S(2)}, u32[]{:S(2)}) collective-permute-start(bf16[640,640]{1,0:T(8,128)(2,1)} %collective-permute-done.1.refs_9_), channel_id=1, source_target_pairs={{0,8},{8,0},{1,9},{9,1},{2,10},{10,2},{3,11},{11,3},{4,12},{12,4},... | collective-permute-start | bytes 2457608 | tf_op jit(solution)/shard_map/ppermute | solution.py:22
  55.1 9.0 %collective-permute-start.4 = (bf16[640,640]{1,0:T(8,128)(2,1)}, bf16[640,640]{1,0:T(8,128)(2,1)}, u32[]{:S(2)}, u32[]{:S(2)}) collective-permute-start(bf16[640,640]{1,0:T(8,128)(2,1)} %collective-permute-done.3.refs_10_), channel_id=1, source_target_pairs={{0,8},{8,0},{1,9},{9,1},{2,10},{10,2},{3,11},{11,3},{4,12},{12,4},... | collective-permute-start | bytes 2457608 | tf_op jit(solution)/shard_map/ppermute | solution.py:22
  55.5 8.6 %collective-permute-start.6 = (bf16[640,640]{1,0:T(8,128)(2,1)S(1)}, bf16[640,640]{1,0:T(8,128)(2,1)}, u32[]{:S(2)}, u32[]{:S(2)}) collective-permute-start(bf16[640,640]{1,0:T(8,128)(2,1)S(1)} %collective-permute-done.5.refs_13_), channel_id=1, source_target_pairs={{0,8},{8,0},{1,9},{9,1},{2,10},{10,2},{3,11},{11,3},{4,12},{12,4},... | collective-permute-start | bytes 2457608 | tf_op jit(solution)/shard_map/ppermute | solution.py:22
  55.6 6.6 %copy-start.7 = (bf16[5120]{0:T(1024)(128)(2,1)S(1)}, bf16[5120]{0:T(1024)(128)(2,1)}, u32[]{:S(2)}) copy-start(bf16[5120]{0:T(1024)(128)(2,1)} %param.20) | copy-start | bytes 30724
  55.6 7.2 %copy-start.8 = (bf16[5120]{0:T(1024)(128)(2,1)S(1)}, bf16[5120]{0:T(1024)(128)(2,1)}, u32[]{:S(2)}) copy-start(bf16[5120]{0:T(1024)(128)(2,1)} %param.21) | copy-start | bytes 30724
  55.6 30.0 %collective-permute-start.9 = (bf16[640,640]{1,0:T(8,128)(2,1)}, bf16[640,640]{1,0:T(8,128)(2,1)}, u32[]{:S(2)}, u32[]{:S(2)}) collective-permute-start(bf16[640,640]{1,0:T(8,128)(2,1)} %collective-permute-done.7.refs_14_), channel_id=1, source_target_pairs={{1,64},{64,1},{65,0},{0,65},{3,66},{66,3},{67,2},{2,67},{5,68},{68... | collective-permute-start | bytes 2457608 | tf_op jit(solution)/shard_map/ppermute | solution.py:26
  59.4 55.3 %collective-permute-start.18 = (bf16[640,1920]{1,0:T(8,128)(2,1)S(1)}, bf16[640,1920]{1,0:T(8,128)(2,1)}, u32[]{:S(2)}, u32[]{:S(2)}) collective-permute-start(bf16[640,1920]{1,0:T(8,128)(2,1)S(1)} %constant_dynamic-slice_fusion), channel_id=1, source_target_pairs={{0,2},{2,4},{4,6},{6,0},{1,3},{3,5},{5,7},{7,1},{8,10},{10,12},{12... | collective-permute-start | bytes 7372808 | tf_op jit(solution)/shard_map/ppermute | solution.py:22
  60.9 53.8 %collective-permute-start.19 = (bf16[640,1920]{1,0:T(8,128)(2,1)S(1)}, bf16[640,1920]{1,0:T(8,128)(2,1)}, u32[]{:S(2)}, u32[]{:S(2)}) collective-permute-start(bf16[640,1920]{1,0:T(8,128)(2,1)S(1)} %constant_dynamic-slice_fusion), channel_id=1, source_target_pairs={{0,6},{2,0},{4,2},{6,4},{1,7},{3,1},{5,3},{7,5},{8,14},{10,8},{12,... | collective-permute-start | bytes 7372808 | tf_op jit(solution)/shard_map/ppermute | solution.py:22
  85.6 2.5 %collective-permute-start.10 = (bf16[640,640]{1,0:T(8,128)(2,1)}, bf16[640,640]{1,0:T(8,128)(2,1)S(1)}, u32[]{:S(2)}, u32[]{:S(2)}) collective-permute-start(bf16[640,640]{1,0:T(8,128)(2,1)} %collective-permute-done.7.refs_14_), channel_id=1, source_target_pairs={{0,8},{8,0},{1,9},{9,1},{2,10},{10,2},{3,11},{11,3},{4,12},{12,4},... | collective-permute-start | bytes 2457608 | tf_op jit(solution)/shard_map/ppermute | solution.py:22
  85.9 16.0 %collective-permute-start.11 = (bf16[640,640]{1,0:T(8,128)(2,1)}, bf16[640,640]{1,0:T(8,128)(2,1)}, u32[]{:S(2)}, u32[]{:S(2)}) collective-permute-start(bf16[640,640]{1,0:T(8,128)(2,1)} %collective-permute-done.8.refs_15_), channel_id=1, source_target_pairs={{0,8},{8,0},{1,9},{9,1},{2,10},{10,2},{3,11},{11,3},{4,12},{12,4},... | collective-permute-start | bytes 2457608 | tf_op jit(solution)/shard_map/ppermute | solution.py:22
  86.1 15.7 %collective-permute-start.12 = (bf16[640,640]{1,0:T(8,128)(2,1)}, bf16[640,640]{1,0:T(8,128)(2,1)}, u32[]{:S(2)}, u32[]{:S(2)}) collective-permute-start(bf16[640,640]{1,0:T(8,128)(2,1)} %collective-permute-done.9.refs_16_), channel_id=1, source_target_pairs={{0,8},{8,0},{1,9},{9,1},{2,10},{10,2},{3,11},{11,3},{4,12},{12,4},... | collective-permute-start | bytes 2457608 | tf_op jit(solution)/shard_map/ppermute | solution.py:22
  88.1 13.7 %copy-start.2 = (bf16[640,640]{1,0:T(8,128)(2,1)}, bf16[640,640]{1,0:T(8,128)(2,1)S(1)}, u32[]{:S(2)}) copy-start(bf16[640,640]{1,0:T(8,128)(2,1)S(1)} %collective-permute-done.10.refs_22_) | copy-start | bytes 2457604
  88.2 21.8 %collective-permute-start.14 = (bf16[4,336,256]{2,1,0:T(8,128)(2,1)}, bf16[4,336,256]{2,1,0:T(8,128)(2,1)}, u32[]{:S(2)}, u32[]{:S(2)}) collective-permute-start(bf16[4,336,256]{2,1,0:T(8,128)(2,1)} %shard_map.123), channel_id=1, source_target_pairs={{0,64},{64,0},{1,65},{65,1},{2,66},{66,2},{3,67},{67,3},{4,68},{68... | collective-permute-start | bytes 2064392 | tf_op jit(solution)/shard_map/ppermute | solution.py:22
  109.2 5.7 %collective-permute-start.13 = (bf16[1,336,256]{2,1,0:T(8,128)(2,1)}, bf16[1,336,256]{2,1,0:T(8,128)(2,1)S(1)}, u32[]{:S(2)}, u32[]{:S(2)}) collective-permute-start(bf16[1,336,256]{2,1,0:T(8,128)(2,1)} %get-tuple-element.42), channel_id=1, source_target_pairs={{0,64},{64,0},{1,65},{65,1},{2,66},{66,2},{3,67},{67,3},{4,68},{68... | collective-permute-start | bytes 516104 | tf_op jit(solution)/shard_map/ppermute | solution.py:22
  115.0 1.9 %copy-start.6 = (bf16[1,336,256]{2,1,0:T(8,128)(2,1)}, bf16[1,336,256]{2,1,0:T(8,128)(2,1)S(1)}, u32[]{:S(2)}) copy-start(bf16[1,336,256]{2,1,0:T(8,128)(2,1)S(1)} %collective-permute-done.13.far_ref) | copy-start | bytes 516100
  115.0 17.4 %collective-permute-start.20 = (bf16[640,1920]{1,0:T(8,128)(2,1)}, bf16[640,1920]{1,0:T(8,128)(2,1)S(1)}, u32[]{:S(2)}, u32[]{:S(2)}) collective-permute-start(bf16[640,1920]{1,0:T(8,128)(2,1)} %collective-permute-done.18.refs_11_), channel_id=1, source_target_pairs={{0,8},{8,0},{1,9},{9,1},{2,10},{10,2},{3,11},{11,3},{4,12},{12,4},... | collective-permute-start | bytes 7372808 | tf_op jit(solution)/shard_map/ppermute | solution.py:22
  116.8 15.6 %collective-permute-start.21 = (bf16[640,1920]{1,0:T(8,128)(2,1)}, bf16[640,1920]{1,0:T(8,128)(2,1)}, u32[]{:S(2)}, u32[]{:S(2)}) collective-permute-start(bf16[640,1920]{1,0:T(8,128)(2,1)} %collective-permute-done.19.refs_12_), channel_id=1, source_target_pairs={{0,8},{8,0},{1,9},{9,1},{2,10},{10,2},{3,11},{11,3},{4,12},{12,4},... | collective-permute-start | bytes 7372808 | tf_op jit(solution)/shard_map/ppermute | solution.py:22
  119.5 7.5 %collective-permute-start.15 = (bf16[2,80,640]{2,1,0:T(8,128)(2,1)}, bf16[2,80,640]{2,1,0:T(8,128)(2,1)S(1)}, u32[]{:S(2)}, u32[]{:S(2)}) collective-permute-start(bf16[2,80,640]{2,1,0:T(8,128)(2,1)} %get-tuple-element.50), channel_id=1, source_target_pairs={{0,2},{2,4},{4,6},{6,0},{1,3},{3,5},{5,7},{7,1},{8,10},{10,12},{12... | collective-permute-start | bytes 614408 | tf_op jit(solution)/shard_map/ppermute | solution.py:22
  120.1 6.9 %collective-permute-start.16 = (bf16[2,80,640]{2,1,0:T(8,128)(2,1)}, bf16[2,80,640]{2,1,0:T(8,128)(2,1)S(1)}, u32[]{:S(2)}, u32[]{:S(2)}) collective-permute-start(bf16[2,80,640]{2,1,0:T(8,128)(2,1)} %get-tuple-element.51), channel_id=1, source_target_pairs={{0,6},{2,0},{4,2},{6,4},{1,7},{3,1},{5,3},{7,5},{8,14},{10,8},{12,... | collective-permute-start | bytes 614408 | tf_op jit(solution)/shard_map/ppermute | solution.py:22
  122.2 10.1 %collective-permute-start.17 = (bf16[2,80,640]{2,1,0:T(8,128)(2,1)}, bf16[2,80,640]{2,1,0:T(8,128)(2,1)S(1)}, u32[]{:S(2)}, u32[]{:S(2)}) collective-permute-start(bf16[2,80,640]{2,1,0:T(8,128)(2,1)} %get-tuple-element.52), channel_id=1, source_target_pairs={{0,4},{2,6},{4,0},{6,2},{1,5},{3,7},{5,1},{7,3},{8,12},{10,14},{12... | collective-permute-start | bytes 614408 | tf_op jit(solution)/shard_map/ppermute | solution.py:22
  127.0 5.4 %copy-start.3 = (bf16[2,80,640]{2,1,0:T(8,128)(2,1)}, bf16[2,80,640]{2,1,0:T(8,128)(2,1)S(1)}, u32[]{:S(2)}) copy-start(bf16[2,80,640]{2,1,0:T(8,128)(2,1)S(1)} %collective-permute-done.15.refs_1_) | copy-start | bytes 614404
  127.0 5.4 %copy-start.4 = (bf16[2,80,640]{2,1,0:T(8,128)(2,1)}, bf16[2,80,640]{2,1,0:T(8,128)(2,1)S(1)}, u32[]{:S(2)}) copy-start(bf16[2,80,640]{2,1,0:T(8,128)(2,1)S(1)} %collective-permute-done.16.refs_2_) | copy-start | bytes 614404
  132.4 0.7 copy-start.5
  132.4 1.5 copy-start
Sparse Core Ops, SparseCore 0:
  10.8 62.3 all-gather.4
  74.9 26.4 all-gather.6
